TPU v7x, 256 devices: a whole 4x4x8 slice. The times are simulated.
256 devices in a mesh: pipe: 16 (over z, x_lo), expert: 16 (over x_hi, y, core).
Axes of the slice: x: 4 (x_hi: 2, x_lo: 2; x = x_hi * 2 + x_lo), y: 4, z: 8, core: 2. Of those that a mesh axis runs over, the one named last changes fastest.
Arguments:
- forward_in: bfloat16 [16, 256, 7168], P('pipe', 'expert'), may hold values from -6 to 6
- forward_route: int32 [16, 256], P('pipe', 'expert'), may hold values from 0 to 1, as said below
- backward_in: bfloat16 [16, 256, 7168], P('pipe', 'expert'), may hold values from -6 to 6
- backward_route: int32 [16, 256], P('pipe', 'expert'), may hold values from 0 to 1, as said below
- backward_grad: bfloat16 [16, 256, 7168], P('pipe', 'expert'), may hold values from -6 to 6
- router: bfloat16 [16, 7168, 2], P('pipe'), may hold values from -0.125 to 0.125
- gate_weight: bfloat16 [16, 7168, 4096], P('pipe', None, 'expert'), may hold values from -0.0625 to 0.0625
- up_weight: bfloat16 [16, 7168, 4096], P('pipe', None, 'expert'), may hold values from -0.0625 to 0.0625
- down_weight: bfloat16 [16, 4096, 7168], P('pipe', 'expert'), may hold values from -0.125 to 0.125
Outputs:
- forward_next: bfloat16 [16, 256, 7168], P('pipe', 'expert')
- backward_out: bfloat16 [16, 256, 7168], P('pipe', 'expert')
Inputs may be any that keep to these rules, and one draw needn't show every extreme that they name: `forward_route`: in every section's micro-batch each expert is named by exactly 128 tokens. `backward_route`: in every section's micro-batch each expert is named by exactly 128 tokens.
All inputs are finite; a program needn't handle non-finite values.
Results may differ from a plain program's by a relative error of at most 0.014.
Values may be sent and summed in bfloat16 or wider, within the bound.
No kernel may reach another device: no remote copies, remote signals or barrier semaphores. Data moves between devices by JAX's collectives and lax.ppermute only.
A program may use at most 128 MiB of HBM per device.

v0:
```python
import functools

import jax
import jax.numpy as jnp
from jax import lax
from jax.experimental import pallas as pl
from jax.experimental.pallas import tpu as pltpu
from jax.sharding import PartitionSpec as P

COLUMNS = 2
CHIPS = 4
CORES = 2
TILE = 1024
LANES = 128
F32 = jnp.float32
BF16 = jnp.bfloat16


def place(column, chip, core):
    return (column * CHIPS + chip % CHIPS) * CORES + core


def moved(block, step):
    pairs = []
    for column in range(COLUMNS):
        for chip in range(CHIPS):
            for core in range(CORES):
                pairs.append((place(column, chip, core), place(*step(column, chip, core))))
    return lax.ppermute(block, "expert", pairs)


def other_column(block):
    return moved(block, lambda column, chip, core: (1 - column, chip, core))


def other_core(block):
    return moved(block, lambda column, chip, core: (column, chip, 1 - core))


def onward(block):
    return moved(block, lambda column, chip, core: (column, chip + 1 - 2 * core, core))


def backward(block):
    return moved(block, lambda column, chip, core: (column, chip - 1 + 2 * core, core))


def to_home(block, distance, cross):
    sections = lax.axis_size("pipe")
    width = COLUMNS * CHIPS * CORES
    pairs = []
    for section in range(sections):
        there = (section + distance) % sections
        for column in range(COLUMNS):
            for chip in range(CHIPS):
                for core in range(CORES):
                    target = 1 - column if cross else column
                    pairs.append(
                        (
                            section * width + place(column, chip, core),
                            there * width + place(target, chip, core),
                        )
                    )
    return lax.ppermute(block, ("pipe", "expert"), pairs)


def collect(own, cross):
    piece = jnp.concatenate([own, other_column(cross)], axis=0)
    pieces, swapped = [piece], [other_core(piece)]
    for _ in range(CHIPS - 1):
        piece = onward(piece)
        pieces.append(piece)
        swapped.append(other_core(piece))
    return pieces, swapped


def give_back(mine, other):
    total = None
    for j in reversed(range(CHIPS)):
        both = mine[j].astype(F32) + other_core(other[j]).astype(F32)
        if total is not None:
            both = both + backward(total.astype(BF16)).astype(F32)
        total = both
    return total


def dot(left, right):
    return jnp.dot(left, right, preferred_element_type=F32)


def dot_turned(left, right):
    return lax.dot_general(left, right, (((1,), (1,)), ((), ())), preferred_element_type=F32)


def lane_sums(x, row):
    total = jnp.zeros((x.shape[0], LANES), F32)
    for start in range(0, x.shape[1], LANES):
        part = x[:, start : start + LANES].astype(F32)
        total = total + part * row[:, start : start + LANES]
    return total


def sigmoid(values):
    return 1.0 / (1.0 + jnp.exp(-values))


def forward_kernel(count, steps, *refs):
    x_refs = refs[:count]
    gate_ref, up_ref, down_ref, router_ref = refs[count : count + 4]
    out_refs = refs[count + 4 : 2 * count + 4]
    gate_acc, up_acc, logit_acc, hidden, gates = refs[2 * count + 4 :]
    i = pl.program_id(0)

    @pl.when(i == 0)
    def _():
        gate_acc[...] = jnp.zeros_like(gate_acc)
        up_acc[...] = jnp.zeros_like(up_acc)
        logit_acc[...] = jnp.zeros_like(logit_acc)

    @pl.when(i < steps)
    def _():
        x = jnp.concatenate([ref[...] for ref in x_refs], axis=0)
        gate_acc[...] += dot(x, gate_ref[...])
        up_acc[...] += dot(x, up_ref[...])
        logit_acc[...] += lane_sums(x, router_ref[...])

    @pl.when(i == steps)
    def _():
        gates[...] = sigmoid(jnp.sum(logit_acc[...], axis=1, keepdims=True))
        gate_pre = gate_acc[...]
        hidden[...] = (gate_pre * sigmoid(gate_pre) * up_acc[...]).astype(BF16)

    @pl.when(i >= steps)
    def _():
        part = (gates[...] * dot(hidden[...], down_ref[...])).astype(BF16)
        rows = part.shape[0] // count
        for j, ref in enumerate(out_refs):
            ref[...] = part[j * rows : (j + 1) * rows]


def backward_kernel(count, steps, *refs):
    x_refs = refs[:count]
    gate_ref, up_ref, down_ref, router_ref = refs[count : count + 4]
    out_refs = refs[count + 4 : 2 * count + 4]
    gate_acc, up_acc, down_acc, logit_acc, gate_slope, up_slope, weight = refs[2 * count + 4 :]
    i = pl.program_id(0)

    @pl.when(i == 0)
    def _():
        gate_acc[...] = jnp.zeros_like(gate_acc)
        up_acc[...] = jnp.zeros_like(up_acc)
        down_acc[...] = jnp.zeros_like(down_acc)
        logit_acc[...] = jnp.zeros_like(logit_acc)

    @pl.when(i < steps)
    def _():
        rows = x_refs[0].shape[0] // 2
        x = jnp.concatenate([ref[:rows] for ref in x_refs], axis=0)
        grad = jnp.concatenate([ref[rows:] for ref in x_refs], axis=0)
        gate_acc[...] += dot(x, gate_ref[...])
        up_acc[...] += dot(x, up_ref[...])
        down_acc[...] += dot_turned(grad, down_ref[...])
        logit_acc[...] += lane_sums(x, router_ref[...])

    @pl.when(i == steps)
    def _():
        gates = sigmoid(jnp.sum(logit_acc[...], axis=1, keepdims=True))
        gate_pre = gate_acc[...]
        up_pre = up_acc[...]
        logistic = sigmoid(gate_pre)
        activated = gate_pre * logistic
        down_slope = gates * down_acc[...]
        hidden = (activated * up_pre).astype(BF16).astype(F32)
        weight[...] = jnp.sum(hidden * down_slope, axis=1, keepdims=True) * (1.0 - gates)
        slope = logistic * (1.0 + gate_pre * (1.0 - logistic))
        gate_slope[...] = (down_slope * up_pre * slope).astype(BF16)
        up_slope[...] = (down_slope * activated).astype(BF16)

    @pl.when(i >= steps)
    def _():
        through = dot_turned(gate_slope[...], gate_ref[...])
        through += dot_turned(up_slope[...], up_ref[...])
        part = (through + weight[...] * router_ref[...]).astype(BF16)
        rows = part.shape[0] // count
        for j, ref in enumerate(out_refs):
            ref[...] = part[j * rows : (j + 1) * rows]


def expert_parts(pieces, gate, up, down, router_row, is_backward):
    model, hidden_units = gate.shape
    steps = model // TILE
    count = len(pieces)
    per_piece = pieces[0].shape[0]
    token_rows = per_piece // 2 if is_backward else per_piece
    rows = token_rows * count

    def first(i):
        return jnp.minimum(i, steps - 1)

    def second(i):
        return jnp.maximum(i - steps, 0)

    def both(i):
        return lax.rem(i, steps)

    if is_backward:
        body = functools.partial(backward_kernel, count, steps)
        weight_at, down_at, router_at = both, first, both
        scratch = [
            pltpu.VMEM((rows, hidden_units), F32),
            pltpu.VMEM((rows, hidden_units), F32),
            pltpu.VMEM((rows, hidden_units), F32),
            pltpu.VMEM((rows, LANES), F32),
            pltpu.VMEM((rows, hidden_units), BF16),
            pltpu.VMEM((rows, hidden_units), BF16),
            pltpu.VMEM((rows, 1), F32),
        ]
    else:
        body = functools.partial(forward_kernel, count, steps)
        weight_at, down_at, router_at = first, second, first
        scratch = [
            pltpu.VMEM((rows, hidden_units), F32),
            pltpu.VMEM((rows, hidden_units), F32),
            pltpu.VMEM((rows, LANES), F32),
            pltpu.VMEM((rows, hidden_units), BF16),
            pltpu.VMEM((rows, 1), F32),
        ]
    products = 5 if is_backward else 3
    return pl.pallas_call(
        body,
        grid=(2 * steps,),
        in_specs=[pl.BlockSpec((per_piece, TILE), lambda i: (0, first(i)))] * count
        + [
            pl.BlockSpec((TILE, hidden_units), lambda i: (weight_at(i), 0)),
            pl.BlockSpec((TILE, hidden_units), lambda i: (weight_at(i), 0)),
            pl.BlockSpec((hidden_units, TILE), lambda i: (0, down_at(i))),
            pl.BlockSpec((1, TILE), lambda i: (0, router_at(i))),
        ],
        out_specs=[pl.BlockSpec((token_rows, TILE), lambda i: (0, second(i)))] * count,
        out_shape=[jax.ShapeDtypeStruct((token_rows, model), BF16)] * count,
        scratch_shapes=scratch,
        compiler_params=pltpu.CompilerParams(vmem_limit_bytes=32 * 1024 * 1024),
        cost_estimate=pl.CostEstimate(
            flops=products * 2 * rows * model * hidden_units,
            bytes_accessed=(products * hidden_units + 2 * rows) * model * 2,
            transcendentals=rows * hidden_units,
        ),
    )(*pieces, gate, up, down, router_row)


def on_device(
    forward_in,
    forward_route,
    backward_in,
    backward_route,
    backward_grad,
    router,
    gate_weight,
    up_weight,
    down_weight,
):
    weights = gate_weight[0], up_weight[0], down_weight[0]
    rows = forward_in.shape[1]
    column = lax.axis_index("expert") // (CHIPS * CORES)
    router_row = jnp.where(column == 0, router[0][:, 0], router[0][:, 1]).astype(F32)[None, :]

    def split(block, route):
        mine = route[0][:, None] == column
        nothing = jnp.zeros((), block.dtype)
        return jnp.where(mine, block[0], nothing), jnp.where(mine, nothing, block[0])

    def finish(base, summed, distance):
        out = (base.astype(F32) + summed).astype(BF16)
        return to_home(out[:rows], distance, False) + to_home(out[rows:], distance, True)

    own, cross = split(forward_in, forward_route)
    forward_rows, forward_swapped = collect(own, cross)
    x_own, x_cross = split(backward_in, backward_route)
    grad_own, grad_cross = split(backward_grad, backward_route)
    arrived = other_column(jnp.concatenate([x_cross, grad_cross], axis=0))
    piece = jnp.concatenate([x_own, arrived[:rows], grad_own, arrived[rows:]], axis=0)
    backward_rows, backward_swapped = [piece], [other_core(piece)]
    for _ in range(CHIPS - 1):
        piece = onward(piece)
        backward_rows.append(piece)
        backward_swapped.append(other_core(piece))

    parts = expert_parts(forward_rows + forward_swapped, *weights, router_row, False)
    forward_sum = give_back(parts[:CHIPS], parts[CHIPS:])
    forward_next = finish(forward_rows[0], forward_sum, 1)

    parts = expert_parts(backward_rows + backward_swapped, *weights, router_row, True)
    backward_sum = give_back(parts[:CHIPS], parts[CHIPS:])
    backward_out = finish(backward_rows[0][2 * rows :], backward_sum, -1)
    return (forward_next[None], backward_out[None])


def solution(mesh):
    return jax.shard_map(
        on_device,
        mesh=mesh,
        in_specs=(
            P("pipe", "expert", None),
            P("pipe", "expert"),
            P("pipe", "expert", None),
            P("pipe", "expert"),
            P("pipe", "expert", None),
            P("pipe", None, None),
            P("pipe", None, "expert"),
            P("pipe", None, "expert"),
            P("pipe", "expert", None),
        ),
        out_specs=(P("pipe", "expert", None), P("pipe", "expert", None)),
        check_vma=False,
    )
```

profile of v0, /device:TPU:4, one launch (start us, length us, event | category | flops | bytes accessed | tf_op | source)
XLA Modules:
  0.0 157.8 jit_solution(3452106312166187544)
XLA Ops:
  2.6 2.3 %collective-permute-start.17 = (bf16[32,7168]{1,0:T(8,128)(2,1)S(1)}, bf16[32,7168]{1,0:T(8,128)(2,1)S(1)}, u32[]{:S(2)}, u32[]{:S(2)}) collective-permute-start(bf16[32,7168]{1,0:T(8,128)(2,1)S(1)} %pad_maximum_fusion.2), channel_id=1, source_target_pairs={{0,8},{1,9},{2,10},{3,11},{4,12},{5,13},{6,14},{7,15},{8,0},{9,1},... | collective-permute-start | bytes 1376264 | tf_op jit(solution)/shard_map/ppermute | solution.py:29
  6.4 11.2 %collective-permute-done.17 = bf16[32,7168]{1,0:T(8,128)(2,1)S(1)} collective-permute-done((bf16[32,7168]{1,0:T(8,128)(2,1)S(1)}, bf16[32,7168]{1,0:T(8,128)(2,1)S(1)}, u32[]{:S(2)}, u32[]{:S(2)}) %collective-permute-start.17) | collective-permute-done | bytes 458784 | tf_op jit(solution)/shard_map/ppermute | solution.py:29
  22.1 1.7 %collective-permute-start.1 = (bf16[32,7168]{1,0:T(8,128)(2,1)S(1)}, bf16[32,7168]{1,0:T(8,128)(2,1)S(1)}, u32[]{:S(2)}, u32[]{:S(2)}) collective-permute-start(bf16[32,7168]{1,0:T(8,128)(2,1)S(1)} %pad_maximum_fusion.1.refs_0_), channel_id=1, source_target_pairs={{0,2},{1,7},{2,4},{3,1},{4,6},{5,3},{6,0},{7,5},{8,10},{9,15},{10,... | collective-permute-start | bytes 1376264 | tf_op jit(solution)/shard_map/ppermute | solution.py:29
  23.7 14.4 %collective-permute-done.1.refs_1_ = bf16[32,7168]{1,0:T(8,128)(2,1)S(1)} collective-permute-done((bf16[32,7168]{1,0:T(8,128)(2,1)S(1)}, bf16[32,7168]{1,0:T(8,128)(2,1)S(1)}, u32[]{:S(2)}, u32[]{:S(2)}) %collective-permute-start.1) | collective-permute-done | bytes 458784 | tf_op jit(solution)/shard_map/ppermute | solution.py:29
  38.5 1.6 collective-permute-start.19
  40.1 7.7 %collective-permute-done.2.refs_2_ = bf16[32,7168]{1,0:T(8,128)(2,1)S(1)} collective-permute-done((bf16[32,7168]{1,0:T(8,128)(2,1)S(1)}, bf16[32,7168]{1,0:T(8,128)(2,1)S(1)}, u32[]{:S(2)}, u32[]{:S(2)}) %collective-permute-start.2) | collective-permute-done | bytes 458784 | tf_op jit(solution)/shard_map/ppermute | solution.py:29
  50.7 11.9 %collective-permute-done.3.refs_3_ = bf16[32,7168]{1,0:T(8,128)(2,1)S(1)} collective-permute-done((bf16[32,7168]{1,0:T(8,128)(2,1)S(1)}, bf16[32,7168]{1,0:T(8,128)(2,1)S(1)}, u32[]{:S(2)}, u32[]{:S(2)}) %collective-permute-start.3) | collective-permute-done | bytes 458784 | tf_op jit(solution)/shard_map/ppermute | solution.py:29
  64.4 2.0 %copy-done = bf16[1,7168,256]{2,1,0:T(8,128)(2,1)S(1)} copy-done((bf16[1,7168,256]{2,1,0:T(8,128)(2,1)S(1)}, bf16[1,7168,256]{2,1,0:T(8,128)(2,1)}, u32[]{:S(2)}) %copy-start) | copy-done | bytes 3670040
  66.5 2.0 %copy-done.2 = bf16[1,7168,256]{2,1,0:T(8,128)(2,1)S(1)} copy-done((bf16[1,7168,256]{2,1,0:T(8,128)(2,1)S(1)}, bf16[1,7168,256]{2,1,0:T(8,128)(2,1)}, u32[]{:S(2)}) %copy-start.2) | copy-done | bytes 3670040
  68.5 2.0 %copy-done.4 = bf16[1,256,7168]{2,1,0:T(8,128)(2,1)S(1)} copy-done((bf16[1,256,7168]{2,1,0:T(8,128)(2,1)S(1)}, bf16[1,256,7168]{2,1,0:T(8,128)(2,1)}, u32[]{:S(2)}) %copy-start.4) | copy-done | bytes 3670040
  74.6 8.8 %shard_map.104 = (bf16[32,7168]{1,0:T(8,128)(2,1)S(1)}, bf16[32,7168]{1,0:T(8,128)(2,1)S(1)}, bf16[32,7168]{1,0:T(8,128)(2,1)S(1)}, bf16[32,7168]{1,0:T(8,128)(2...) custom-call(bf16[32,7168]{1,0:T(8,128)(2,1)S(1)} %copy-done.10, ...), custom_call_target="tpu_custom_call" | custom-call | flops 2818572288 | bytes 18350080 | tf_op jit(solution)/shard_map/pallas_call | solution.py:229
  88.2 2.0 %collective-permute-done.21.refs_4_ = bf16[64,7168]{1,0:T(8,128)(2,1)S(1)} collective-permute-done((bf16[64,7168]{1,0:T(8,128)(2,1)S(1)}, bf16[64,7168]{1,0:T(8,128)(2,1)S(1)}, u32[]{:S(2)}, u32[]{:S(2)}) %collective-permute-start.21) | collective-permute-done | bytes 917536 | tf_op jit(solution)/shard_map/ppermute | solution.py:29
  90.2 2.3 %collective-permute-start.12 = (bf16[32,7168]{1,0:T(8,128)(2,1)S(1)}, bf16[32,7168]{1,0:T(8,128)(2,1)S(1)}, u32[]{:S(2)}, u32[]{:S(2)}) collective-permute-start(bf16[32,7168]{1,0:T(8,128)(2,1)S(1)} %add_convert_fusion.7), channel_id=1, source_target_pairs={{0,6},{1,3},{2,0},{3,5},{4,2},{5,7},{6,4},{7,1},{8,14},{9,11},{10,... | collective-permute-start | bytes 1376264 | tf_op jit(solution)/shard_map/ppermute | solution.py:29
  95.9 11.2 %shard_map.105 = (bf16[32,7168]{1,0:T(8,128)(2,1)S(1)}, bf16[32,7168]{1,0:T(8,128)(2,1)S(1)}, bf16[32,7168]{1,0:T(8,128)(2,1)S(1)}, bf16[32,7168]{1,0:T(8,128)(2...) custom-call(bf16[64,7168]{1,0:T(8,128)(2,1)S(1)} %copy-done.8, ...), custom_call_target="tpu_custom_call" | custom-call | flops 4697620480 | bytes 25690112 | tf_op jit(solution)/shard_map/pallas_call | solution.py:229
  107.5 2.4 %collective-permute-start.13 = (bf16[32,7168]{1,0:T(8,128)(2,1)S(1)}, bf16[32,7168]{1,0:T(8,128)(2,1)S(1)}, u32[]{:S(2)}, u32[]{:S(2)}) collective-permute-start(bf16[32,7168]{1,0:T(8,128)(2,1)S(1)} %add_convert_fusion.6), channel_id=1, source_target_pairs={{0,6},{1,3},{2,0},{3,5},{4,2},{5,7},{6,4},{7,1},{8,14},{9,11},{10,... | collective-permute-start | bytes 1376264 | tf_op jit(solution)/shard_map/ppermute | solution.py:29
  111.5 4.6 %collective-permute-done.13 = bf16[32,7168]{1,0:T(8,128)(2,1)S(1)} collective-permute-done((bf16[32,7168]{1,0:T(8,128)(2,1)S(1)}, bf16[32,7168]{1,0:T(8,128)(2,1)S(1)}, u32[]{:S(2)}, u32[]{:S(2)}) %collective-permute-start.13) | collective-permute-done | bytes 458784 | tf_op jit(solution)/shard_map/ppermute | solution.py:29
  116.2 3.6 %collective-permute-start.14 = (bf16[32,7168]{1,0:T(8,128)(2,1)S(1)}, bf16[32,7168]{1,0:T(8,128)(2,1)S(1)}, u32[]{:S(2)}, u32[]{:S(2)}) collective-permute-start(bf16[32,7168]{1,0:T(8,128)(2,1)S(1)} %add_convert_fusion.5), channel_id=1, source_target_pairs={{0,6},{1,3},{2,0},{3,5},{4,2},{5,7},{6,4},{7,1},{8,14},{9,11},{10,... | collective-permute-start | bytes 1376264 | tf_op jit(solution)/shard_map/ppermute | solution.py:29
  121.1 3.6 %collective-permute-start.30 = (bf16[32,7168]{1,0:T(8,128)(2,1)S(1)}, bf16[32,7168]{1,0:T(8,128)(2,1)S(1)}, u32[]{:S(2)}, u32[]{:S(2)}) collective-permute-start(bf16[32,7168]{1,0:T(8,128)(2,1)S(1)} %add_convert_fusion.2), channel_id=1, source_target_pairs={{0,6},{1,3},{2,0},{3,5},{4,2},{5,7},{6,4},{7,1},{8,14},{9,11},{10,... | collective-permute-start | bytes 1376264 | tf_op jit(solution)/shard_map/ppermute | solution.py:29
  126.7 4.1 %collective-permute-done.30 = bf16[32,7168]{1,0:T(8,128)(2,1)S(1)} collective-permute-done((bf16[32,7168]{1,0:T(8,128)(2,1)S(1)}, bf16[32,7168]{1,0:T(8,128)(2,1)S(1)}, u32[]{:S(2)}, u32[]{:S(2)}) %collective-permute-start.30) | collective-permute-done | bytes 458784 | tf_op jit(solution)/shard_map/ppermute | solution.py:29
  131.0 3.7 %collective-permute-start.31 = (bf16[32,7168]{1,0:T(8,128)(2,1)S(1)}, bf16[32,7168]{1,0:T(8,128)(2,1)S(1)}, u32[]{:S(2)}, u32[]{:S(2)}) collective-permute-start(bf16[32,7168]{1,0:T(8,128)(2,1)S(1)} %add_convert_fusion.1), channel_id=1, source_target_pairs={{0,6},{1,3},{2,0},{3,5},{4,2},{5,7},{6,4},{7,1},{8,14},{9,11},{10,... | collective-permute-start | bytes 1376264 | tf_op jit(solution)/shard_map/ppermute | solution.py:29
  137.2 3.5 %collective-permute-done.31 = bf16[32,7168]{1,0:T(8,128)(2,1)S(1)} collective-permute-done((bf16[32,7168]{1,0:T(8,128)(2,1)S(1)}, bf16[32,7168]{1,0:T(8,128)(2,1)S(1)}, u32[]{:S(2)}, u32[]{:S(2)}) %collective-permute-start.31) | collective-permute-done | bytes 458784 | tf_op jit(solution)/shard_map/ppermute | solution.py:29
  141.0 6.6 %collective-permute-start.32 = (bf16[16,7168]{1,0:T(8,128)(2,1)S(1)}, bf16[16,7168]{1,0:T(8,128)(2,1)S(1)}, u32[]{:S(2)}, u32[]{:S(2)}) collective-permute-start(bf16[16,7168]{1,0:T(8,128)(2,1)S(1)} %get-tuple-element.35), channel_id=1, source_target_pairs={{0,240},{1,241},{2,242},{3,243},{4,244},{5,245},{6,246},{7,247},{8... | collective-permute-start | bytes 688136 | tf_op jit(solution)/shard_map/ppermute | solution.py:64
  148.8 4.7 %collective-permute-done.32 = bf16[16,7168]{1,0:T(8,128)(2,1)S(1)} collective-permute-done((bf16[16,7168]{1,0:T(8,128)(2,1)S(1)}, bf16[16,7168]{1,0:T(8,128)(2,1)S(1)}, u32[]{:S(2)}, u32[]{:S(2)}) %collective-permute-start.32) | collective-permute-done | bytes 229408 | tf_op jit(solution)/shard_map/ppermute | solution.py:64
  153.6 3.5 %collective-permute-done.33 = bf16[16,7168]{1,0:T(8,128)(2,1)S(1)} collective-permute-done((bf16[16,7168]{1,0:T(8,128)(2,1)S(1)}, bf16[16,7168]{1,0:T(8,128)(2,1)S(1)}, u32[]{:S(2)}, u32[]{:S(2)}) %collective-permute-start.33) | collective-permute-done | bytes 229408 | tf_op jit(solution)/shard_map/ppermute | solution.py:64
  (138 shorter events, 35.3 us)
Async XLA Ops:
  2.6 15.0 %collective-permute-start.17 = (bf16[32,7168]{1,0:T(8,128)(2,1)S(1)}, bf16[32,7168]{1,0:T(8,128)(2,1)S(1)}, u32[]{:S(2)}, u32[]{:S(2)}) collective-permute-start(bf16[32,7168]{1,0:T(8,128)(2,1)S(1)} %pad_maximum_fusion.2), channel_id=1, source_target_pairs={{0,8},{1,9},{2,10},{3,11},{4,12},{5,13},{6,14},{7,15},{8,0},{9,1},... | collective-permute-start | bytes 1376264 | tf_op jit(solution)/shard_map/ppermute | solution.py:29
  5.1 16.3 %collective-permute-start = (bf16[16,7168]{1,0:T(8,128)(2,1)S(1)}, bf16[16,7168]{1,0:T(8,128)(2,1)S(1)}, u32[]{:S(2)}, u32[]{:S(2)}) collective-permute-start(bf16[16,7168]{1,0:T(8,128)(2,1)S(1)} %get-tuple-element.45), channel_id=1, source_target_pairs={{0,8},{1,9},{2,10},{3,11},{4,12},{5,13},{6,14},{7,15},{8,0},{9,1},... | collective-permute-start | bytes 688136 | tf_op jit(solution)/shard_map/ppermute | solution.py:29
  18.7 19.9 %collective-permute-start.18 = (bf16[64,7168]{1,0:T(8,128)(2,1)S(1)}, bf16[64,7168]{1,0:T(8,128)(2,1)S(1)}, u32[]{:S(2)}, u32[]{:S(2)}) collective-permute-start(bf16[64,7168]{1,0:T(8,128)(2,1)S(1)} %pad_maximum_fusion.refs_0_), channel_id=1, source_target_pairs={{0,2},{1,7},{2,4},{3,1},{4,6},{5,3},{6,0},{7,5},{8,10},{9,15},{10,... | collective-permute-start | bytes 2752520 | tf_op jit(solution)/shard_map/ppermute | solution.py:29
  22.1 16.1 %collective-permute-start.1 = (bf16[32,7168]{1,0:T(8,128)(2,1)S(1)}, bf16[32,7168]{1,0:T(8,128)(2,1)S(1)}, u32[]{:S(2)}, u32[]{:S(2)}) collective-permute-start(bf16[32,7168]{1,0:T(8,128)(2,1)S(1)} %pad_maximum_fusion.1.refs_0_), channel_id=1, source_target_pairs={{0,2},{1,7},{2,4},{3,1},{4,6},{5,3},{6,0},{7,5},{8,10},{9,15},{10,... | collective-permute-start | bytes 1376264 | tf_op jit(solution)/shard_map/ppermute | solution.py:29
  38.2 9.7 %collective-permute-start.2 = (bf16[32,7168]{1,0:T(8,128)(2,1)S(1)}, bf16[32,7168]{1,0:T(8,128)(2,1)S(1)}, u32[]{:S(2)}, u32[]{:S(2)}) collective-permute-start(bf16[32,7168]{1,0:T(8,128)(2,1)S(1)} %collective-permute-done.1.refs_1_), channel_id=1, source_target_pairs={{0,2},{1,7},{2,4},{3,1},{4,6},{5,3},{6,0},{7,5},{8,10},{9,15},{10,... | collective-permute-start | bytes 1376264 | tf_op jit(solution)/shard_map/ppermute | solution.py:29
  38.5 24.9 %collective-permute-start.19 = (bf16[64,7168]{1,0:T(8,128)(2,1)S(1)}, bf16[64,7168]{1,0:T(8,128)(2,1)}, u32[]{:S(2)}, u32[]{:S(2)}) collective-permute-start(bf16[64,7168]{1,0:T(8,128)(2,1)S(1)} %collective-permute-done.18.refs_1_), channel_id=1, source_target_pairs={{0,2},{1,7},{2,4},{3,1},{4,6},{5,3},{6,0},{7,5},{8,10},{9,15},{10,... | collective-permute-start | bytes 2752520 | tf_op jit(solution)/shard_map/ppermute | solution.py:29
  47.9 14.7 %collective-permute-start.3 = (bf16[32,7168]{1,0:T(8,128)(2,1)S(1)}, bf16[32,7168]{1,0:T(8,128)(2,1)S(1)}, u32[]{:S(2)}, u32[]{:S(2)}) collective-permute-start(bf16[32,7168]{1,0:T(8,128)(2,1)S(1)} %collective-permute-done.2.refs_2_), channel_id=1, source_target_pairs={{0,2},{1,7},{2,4},{3,1},{4,6},{5,3},{6,0},{7,5},{8,10},{9,15},{10,... | collective-permute-start | bytes 1376264 | tf_op jit(solution)/shard_map/ppermute | solution.py:29
  47.9 15.6 %collective-permute-start.4 = (bf16[32,7168]{1,0:T(8,128)(2,1)S(1)}, bf16[32,7168]{1,0:T(8,128)(2,1)S(1)}, u32[]{:S(2)}, u32[]{:S(2)}) collective-permute-start(bf16[32,7168]{1,0:T(8,128)(2,1)S(1)} %pad_maximum_fusion.1.refs_0_), channel_id=1, source_target_pairs={{0,1},{1,0},{2,3},{3,2},{4,5},{5,4},{6,7},{7,6},{8,9},{9,8},{10,11... | collective-permute-start | bytes 1376264 | tf_op jit(solution)/shard_map/ppermute | solution.py:29
  48.7 14.8 %collective-permute-start.5 = (bf16[32,7168]{1,0:T(8,128)(2,1)S(1)}, bf16[32,7168]{1,0:T(8,128)(2,1)S(1)}, u32[]{:S(2)}, u32[]{:S(2)}) collective-permute-start(bf16[32,7168]{1,0:T(8,128)(2,1)S(1)} %collective-permute-done.1.refs_1_), channel_id=1, source_target_pairs={{0,1},{1,0},{2,3},{3,2},{4,5},{5,4},{6,7},{7,6},{8,9},{9,8},{10,11... | collective-permute-start | bytes 1376264 | tf_op jit(solution)/shard_map/ppermute | solution.py:29
  49.9 13.6 %collective-permute-start.6 = (bf16[32,7168]{1,0:T(8,128)(2,1)S(1)}, bf16[32,7168]{1,0:T(8,128)(2,1)S(1)}, u32[]{:S(2)}, u32[]{:S(2)}) collective-permute-start(bf16[32,7168]{1,0:T(8,128)(2,1)S(1)} %collective-permute-done.2.refs_2_), channel_id=1, source_target_pairs={{0,1},{1,0},{2,3},{3,2},{4,5},{5,4},{6,7},{7,6},{8,9},{9,8},{10,11... | collective-permute-start | bytes 1376264 | tf_op jit(solution)/shard_map/ppermute | solution.py:29
  63.4 24.3 %collective-permute-start.20 = (bf16[64,7168]{1,0:T(8,128)(2,1)}, bf16[64,7168]{1,0:T(8,128)(2,1)S(1)}, u32[]{:S(2)}, u32[]{:S(2)}) collective-permute-start(bf16[64,7168]{1,0:T(8,128)(2,1)} %collective-permute-done.19.refs_2_), channel_id=1, source_target_pairs={{0,2},{1,7},{2,4},{3,1},{4,6},{5,3},{6,0},{7,5},{8,10},{9,15},{10,... | collective-permute-start | bytes 2752520 | tf_op jit(solution)/shard_map/ppermute | solution.py:29
  86.4 20.8 %collective-permute-start.10 = (bf16[32,7168]{1,0:T(8,128)(2,1)}, bf16[32,7168]{1,0:T(8,128)(2,1)S(1)}, u32[]{:S(2)}, u32[]{:S(2)}) collective-permute-start(bf16[32,7168]{1,0:T(8,128)(2,1)} %get-tuple-element.23), channel_id=1, source_target_pairs={{0,1},{1,0},{2,3},{3,2},{4,5},{5,4},{6,7},{7,6},{8,9},{9,8},{10,11... | collective-permute-start | bytes 1376264 | tf_op jit(solution)/shard_map/ppermute | solution.py:29
  90.2 17.1 %collective-permute-start.12 = (bf16[32,7168]{1,0:T(8,128)(2,1)S(1)}, bf16[32,7168]{1,0:T(8,128)(2,1)S(1)}, u32[]{:S(2)}, u32[]{:S(2)}) collective-permute-start(bf16[32,7168]{1,0:T(8,128)(2,1)S(1)} %add_convert_fusion.7), channel_id=1, source_target_pairs={{0,6},{1,3},{2,0},{3,5},{4,2},{5,7},{6,4},{7,1},{8,14},{9,11},{10,... | collective-permute-start | bytes 1376264 | tf_op jit(solution)/shard_map/ppermute | solution.py:29
  92.6 18.9 %collective-permute-start.9 = (bf16[32,7168]{1,0:T(8,128)(2,1)}, bf16[32,7168]{1,0:T(8,128)(2,1)S(1)}, u32[]{:S(2)}, u32[]{:S(2)}) collective-permute-start(bf16[32,7168]{1,0:T(8,128)(2,1)} %get-tuple-element.21), channel_id=1, source_target_pairs={{0,1},{1,0},{2,3},{3,2},{4,5},{5,4},{6,7},{7,6},{8,9},{9,8},{10,11... | collective-permute-start | bytes 1376264 | tf_op jit(solution)/shard_map/ppermute | solution.py:29
  92.8 31.9 %collective-permute-start.8 = (bf16[32,7168]{1,0:T(8,128)(2,1)}, bf16[32,7168]{1,0:T(8,128)(2,1)S(1)}, u32[]{:S(2)}, u32[]{:S(2)}) collective-permute-start(bf16[32,7168]{1,0:T(8,128)(2,1)} %get-tuple-element.19), channel_id=1, source_target_pairs={{0,1},{1,0},{2,3},{3,2},{4,5},{5,4},{6,7},{7,6},{8,9},{9,8},{10,11... | collective-permute-start | bytes 1376264 | tf_op jit(solution)/shard_map/ppermute | solution.py:29
  109.9 10.0 %collective-permute-start.27 = (bf16[32,7168]{1,0:T(8,128)(2,1)S(1)}, bf16[32,7168]{1,0:T(8,128)(2,1)S(1)}, u32[]{:S(2)}, u32[]{:S(2)}) collective-permute-start(bf16[32,7168]{1,0:T(8,128)(2,1)S(1)} %get-tuple-element.31), channel_id=1, source_target_pairs={{0,1},{1,0},{2,3},{3,2},{4,5},{5,4},{6,7},{7,6},{8,9},{9,8},{10,11... | collective-permute-start | bytes 1376264 | tf_op jit(solution)/shard_map/ppermute | solution.py:29
  110.0 10.9 %collective-permute-start.29 = (bf16[32,7168]{1,0:T(8,128)(2,1)S(1)}, bf16[32,7168]{1,0:T(8,128)(2,1)S(1)}, u32[]{:S(2)}, u32[]{:S(2)}) collective-permute-start(bf16[32,7168]{1,0:T(8,128)(2,1)S(1)} %add_convert_fusion.3), channel_id=1, source_target_pairs={{0,6},{1,3},{2,0},{3,5},{4,2},{5,7},{6,4},{7,1},{8,14},{9,11},{10,... | collective-permute-start | bytes 1376264 | tf_op jit(solution)/shard_map/ppermute | solution.py:29
  116.2 9.6 %collective-permute-start.14 = (bf16[32,7168]{1,0:T(8,128)(2,1)S(1)}, bf16[32,7168]{1,0:T(8,128)(2,1)S(1)}, u32[]{:S(2)}, u32[]{:S(2)}) collective-permute-start(bf16[32,7168]{1,0:T(8,128)(2,1)S(1)} %add_convert_fusion.5), channel_id=1, source_target_pairs={{0,6},{1,3},{2,0},{3,5},{4,2},{5,7},{6,4},{7,1},{8,14},{9,11},{10,... | collective-permute-start | bytes 1376264 | tf_op jit(solution)/shard_map/ppermute | solution.py:29
  121.1 9.7 %collective-permute-start.30 = (bf16[32,7168]{1,0:T(8,128)(2,1)S(1)}, bf16[32,7168]{1,0:T(8,128)(2,1)S(1)}, u32[]{:S(2)}, u32[]{:S(2)}) collective-permute-start(bf16[32,7168]{1,0:T(8,128)(2,1)S(1)} %add_convert_fusion.2), channel_id=1, source_target_pairs={{0,6},{1,3},{2,0},{3,5},{4,2},{5,7},{6,4},{7,1},{8,14},{9,11},{10,... | collective-permute-start | bytes 1376264 | tf_op jit(solution)/shard_map/ppermute | solution.py:29
  126.1 11.1 %collective-permute-start.25 = (bf16[32,7168]{1,0:T(8,128)(2,1)S(1)}, bf16[32,7168]{1,0:T(8,128)(2,1)S(1)}, u32[]{:S(2)}, u32[]{:S(2)}) collective-permute-start(bf16[32,7168]{1,0:T(8,128)(2,1)S(1)} %get-tuple-element.27), channel_id=1, source_target_pairs={{0,1},{1,0},{2,3},{3,2},{4,5},{5,4},{6,7},{7,6},{8,9},{9,8},{10,11... | collective-permute-start | bytes 1376264 | tf_op jit(solution)/shard_map/ppermute | solution.py:29
  131.0 9.7 %collective-permute-start.31 = (bf16[32,7168]{1,0:T(8,128)(2,1)S(1)}, bf16[32,7168]{1,0:T(8,128)(2,1)S(1)}, u32[]{:S(2)}, u32[]{:S(2)}) collective-permute-start(bf16[32,7168]{1,0:T(8,128)(2,1)S(1)} %add_convert_fusion.1), channel_id=1, source_target_pairs={{0,6},{1,3},{2,0},{3,5},{4,2},{5,7},{6,4},{7,1},{8,14},{9,11},{10,... | collective-permute-start | bytes 1376264 | tf_op jit(solution)/shard_map/ppermute | solution.py:29
  134.7 12.8 %collective-permute-start.15 = (bf16[16,7168]{1,0:T(8,128)(2,1)S(1)}, bf16[16,7168]{1,0:T(8,128)(2,1)S(1)}, u32[]{:S(2)}, u32[]{:S(2)}) collective-permute-start(bf16[16,7168]{1,0:T(8,128)(2,1)S(1)} %get-tuple-element.39), channel_id=1, source_target_pairs={{0,16},{1,17},{2,18},{3,19},{4,20},{5,21},{6,22},{7,23},{8,24},{9,... | collective-permute-start | bytes 688136 | tf_op jit(solution)/shard_map/ppermute | solution.py:64
  136.0 12.1 %collective-permute-start.16 = (bf16[16,7168]{1,0:T(8,128)(2,1)S(1)}, bf16[16,7168]{1,0:T(8,128)(2,1)S(1)}, u32[]{:S(2)}, u32[]{:S(2)}) collective-permute-start(bf16[16,7168]{1,0:T(8,128)(2,1)S(1)} %get-tuple-element.38), channel_id=1, source_target_pairs={{0,24},{1,25},{2,26},{3,27},{4,28},{5,29},{6,30},{7,31},{8,16},{9,... | collective-permute-start | bytes 688136 | tf_op jit(solution)/shard_map/ppermute | solution.py:64
  141.0 12.6 %collective-permute-start.32 = (bf16[16,7168]{1,0:T(8,128)(2,1)S(1)}, bf16[16,7168]{1,0:T(8,128)(2,1)S(1)}, u32[]{:S(2)}, u32[]{:S(2)}) collective-permute-start(bf16[16,7168]{1,0:T(8,128)(2,1)S(1)} %get-tuple-element.35), channel_id=1, source_target_pairs={{0,240},{1,241},{2,242},{3,243},{4,244},{5,245},{6,246},{7,247},{8... | collective-permute-start | bytes 688136 | tf_op jit(solution)/shard_map/ppermute | solution.py:64
  (46 other events, 365.0 us)
where the time goes:
time: 158 us
  waiting for transfers between devices  73.9 us (47%)
  starting transfers between devices  38.3 us (24%)
  Pallas kernels  20 us (13%)
  local copies, waits for them, and re-layouts  19.7 us (12%)
  other arithmetic  4.95 us (3%)
    ppermute x30, waiting for transfers between devices, moved(): return lax.ppermute(block, 'expert', pairs)  65.1 us
    ppermute x30, starting transfers between devices, moved(): return lax.ppermute(block, 'expert', pairs)  29.2 us
    pallas_call x2, Pallas kernels, expert_parts(): pl.pallas_call(body, grid=(2 * steps,), in_specs=[pl.BlockSpec((per_piece...  20 us
    unnamed x72, local copies, waits for them, and re-layouts  19.7 us
    ppermute x4, starting transfers between devices, to_home(): return lax.ppermute(block, ('pipe', 'expert'), pairs)  9.06 us
    ppermute x4, waiting for transfers between devices, to_home(): return lax.ppermute(block, ('pipe', 'expert'), pairs)  8.84 us
  transfers between devices with their start and end apart: 34, of which 18 were waited for; matrix products, arithmetic and copies ran while one was open for 2% of the time, Pallas kernels for 13%

commit v1 on v0

--- a/solution.py
+++ b/solution.py
@@ -10,7 +10,7 @@
 COLUMNS = 2
 CHIPS = 4
 CORES = 2
-TILE = 1024
+TILE = 1792
 LANES = 128
 F32 = jnp.float32
 BF16 = jnp.bfloat16
@@ -27,6 +27,10 @@
             for core in range(CORES):
                 pairs.append((place(column, chip, core), place(*step(column, chip, core))))
     return lax.ppermute(block, "expert", pairs)
+
+
+def join(*blocks):
+    return lax.optimization_barrier(blocks)
 
 
 def other_column(block):
@@ -64,23 +68,10 @@
     return lax.ppermute(block, ("pipe", "expert"), pairs)
 
 
-def collect(own, cross):
-    piece = jnp.concatenate([own, other_column(cross)], axis=0)
-    pieces, swapped = [piece], [other_core(piece)]
-    for _ in range(CHIPS - 1):
-        piece = onward(piece)
-        pieces.append(piece)
-        swapped.append(other_core(piece))
-    return pieces, swapped
-
-
-def give_back(mine, other):
-    total = None
-    for j in reversed(range(CHIPS)):
-        both = mine[j].astype(F32) + other_core(other[j]).astype(F32)
-        if total is not None:
-            both = both + backward(total.astype(BF16)).astype(F32)
-        total = both
+def summed(mine, *others):
+    total = mine.astype(F32)
+    for other in others:
+        total = total + other.astype(F32)
     return total
 
 
@@ -105,10 +96,10 @@
 
 
 def forward_kernel(count, steps, *refs):
-    x_refs = refs[:count]
-    gate_ref, up_ref, down_ref, router_ref = refs[count : count + 4]
-    out_refs = refs[count + 4 : 2 * count + 4]
-    gate_acc, up_acc, logit_acc, hidden, gates = refs[2 * count + 4 :]
+    x_refs, route_refs = refs[:count], refs[count : 2 * count]
+    gate_ref, up_ref, down_ref, router_ref, column_ref = refs[2 * count : 2 * count + 5]
+    out_refs = refs[2 * count + 5 : 3 * count + 5]
+    gate_acc, up_acc, logit_acc, hidden, gates = refs[3 * count + 5 :]
     i = pl.program_id(0)
 
     @pl.when(i == 0)
@@ -127,8 +118,11 @@
     @pl.when(i == steps)
     def _():
         gates[...] = sigmoid(jnp.sum(logit_acc[...], axis=1, keepdims=True))
+        routes = jnp.concatenate([ref[...] for ref in route_refs], axis=0).astype(F32)
+        mask = (routes == column_ref[...]).astype(F32)
+        mask = jnp.concatenate([mask] * (hidden.shape[1] // LANES), axis=1)
         gate_pre = gate_acc[...]
-        hidden[...] = (gate_pre * sigmoid(gate_pre) * up_acc[...]).astype(BF16)
+        hidden[...] = (gate_pre * sigmoid(gate_pre) * up_acc[...] * mask).astype(BF16)
 
     @pl.when(i >= steps)
     def _():
@@ -186,7 +180,7 @@
             ref[...] = part[j * rows : (j + 1) * rows]
 
 
-def expert_parts(pieces, gate, up, down, router_row, is_backward):
+def expert_parts(pieces, gate, up, down, router_row, column_row, is_backward):
     model, hidden_units = gate.shape
     steps = model // TILE
     count = len(pieces)
@@ -226,26 +220,40 @@
             pltpu.VMEM((rows, 1), F32),
         ]
     products = 5 if is_backward else 3
+    route_specs = [pl.BlockSpec((per_piece, LANES), lambda i: (0, model // LANES))] * count
+    gate, up, down = (
+        pltpu.with_memory_space_constraint(weight, pltpu.HBM) for weight in (gate, up, down)
+    )
     return pl.pallas_call(
         body,
         grid=(2 * steps,),
         in_specs=[pl.BlockSpec((per_piece, TILE), lambda i: (0, first(i)))] * count
+        + ([] if is_backward else route_specs)
         + [
             pl.BlockSpec((TILE, hidden_units), lambda i: (weight_at(i), 0)),
             pl.BlockSpec((TILE, hidden_units), lambda i: (weight_at(i), 0)),
             pl.BlockSpec((hidden_units, TILE), lambda i: (0, down_at(i))),
             pl.BlockSpec((1, TILE), lambda i: (0, router_at(i))),
-        ],
+        ]
+        + ([] if is_backward else [pl.BlockSpec((1, LANES), lambda i: (0, 0))]),
         out_specs=[pl.BlockSpec((token_rows, TILE), lambda i: (0, second(i)))] * count,
         out_shape=[jax.ShapeDtypeStruct((token_rows, model), BF16)] * count,
         scratch_shapes=scratch,
-        compiler_params=pltpu.CompilerParams(vmem_limit_bytes=32 * 1024 * 1024),
+        compiler_params=pltpu.CompilerParams(vmem_limit_bytes=24 * 1024 * 1024),
         cost_estimate=pl.CostEstimate(
             flops=products * 2 * rows * model * hidden_units,
             bytes_accessed=(products * hidden_units + 2 * rows) * model * 2,
             transcendentals=rows * hidden_units,
         ),
-    )(*pieces, gate, up, down, router_row)
+    )(
+        *pieces,
+        *([] if is_backward else pieces),
+        gate,
+        up,
+        down,
+        router_row,
+        *([] if is_backward else [column_row]),
+    )
 
 
 def on_device(
@@ -264,34 +272,64 @@
     column = lax.axis_index("expert") // (CHIPS * CORES)
     router_row = jnp.where(column == 0, router[0][:, 0], router[0][:, 1]).astype(F32)[None, :]
 
+    column_row = jnp.full((1, LANES), column, F32)
+
     def split(block, route):
         mine = route[0][:, None] == column
         nothing = jnp.zeros((), block.dtype)
         return jnp.where(mine, block[0], nothing), jnp.where(mine, nothing, block[0])
 
-    def finish(base, summed, distance):
-        out = (base.astype(F32) + summed).astype(BF16)
-        return to_home(out[:rows], distance, False) + to_home(out[rows:], distance, True)
-
-    own, cross = split(forward_in, forward_route)
-    forward_rows, forward_swapped = collect(own, cross)
+    def stack(*blocks):
+        return jnp.concatenate(blocks, axis=0)
+
     x_own, x_cross = split(backward_in, backward_route)
     grad_own, grad_cross = split(backward_grad, backward_route)
-    arrived = other_column(jnp.concatenate([x_cross, grad_cross], axis=0))
-    piece = jnp.concatenate([x_own, arrived[:rows], grad_own, arrived[rows:]], axis=0)
-    backward_rows, backward_swapped = [piece], [other_core(piece)]
-    for _ in range(CHIPS - 1):
-        piece = onward(piece)
-        backward_rows.append(piece)
-        backward_swapped.append(other_core(piece))
-
-    parts = expert_parts(forward_rows + forward_swapped, *weights, router_row, False)
-    forward_sum = give_back(parts[:CHIPS], parts[CHIPS:])
-    forward_next = finish(forward_rows[0], forward_sum, 1)
-
-    parts = expert_parts(backward_rows + backward_swapped, *weights, router_row, True)
-    backward_sum = give_back(parts[:CHIPS], parts[CHIPS:])
-    backward_out = finish(backward_rows[0][2 * rows :], backward_sum, -1)
+    lanes = jnp.broadcast_to(forward_route[0].astype(BF16)[:, None], (rows, LANES))
+    f0 = jnp.concatenate([forward_in[0], lanes], axis=1)
+
+    x_arrived, f1 = join(other_column(x_cross), onward(f0))
+    f1, grad_cross = join(f1, grad_cross)
+    grad_arrived, f2 = join(other_column(grad_cross), onward(f1))
+    b0 = stack(x_own, x_arrived, grad_own, grad_arrived)
+    near = stack(f0, f1)
+    b0, near, f2 = join(b0, near, f2)
+    b1, near_crossed, f3 = join(onward(b0), other_column(near), onward(f2))
+    far = stack(f2, f3)
+    b1, far = join(b1, far)
+    b2, far_crossed = join(onward(b1), other_column(far))
+    pieces = [near, far, near_crossed, far_crossed]
+    pieces = pieces + [other_core(piece) for piece in pieces]
+    b2, *pieces = join(b2, *pieces)
+    parts = expert_parts(pieces, *weights, router_row, column_row, False)
+    b3, *parts = join(onward(b2), *parts)
+
+    far_back = summed(parts[3], other_core(parts[7])).astype(BF16)
+    pieces = [b0, b1, b2, b3]
+    pieces = pieces + [other_core(piece) for piece in pieces]
+    far_back, *pieces = join(far_back, *pieces)
+    near_back = summed(parts[2], other_core(parts[6])).astype(BF16)
+    far_here = summed(parts[1], other_core(parts[5]))
+    near_here = summed(parts[0], other_core(parts[4]))
+    b_parts = expert_parts(pieces, *weights, router_row, column_row, True)
+    far_back, near_back, *b_parts = join(other_column(far_back), near_back, *b_parts)
+
+    far_here = summed(far_here, far_back)
+    b_total = summed(b_parts[3], other_core(b_parts[7])).astype(BF16)
+    f_total = far_here[rows:].astype(BF16)
+    near_back, b_total, f_total = join(near_back, b_total, f_total)
+    near_back, f_total = other_column(near_back), backward(f_total)
+    b_total = summed(backward(b_total), b_parts[2], other_core(b_parts[6])).astype(BF16)
+    b_total = summed(backward(b_total), b_parts[1], other_core(b_parts[5])).astype(BF16)
+    b_total, near_back, f_total = join(b_total, near_back, f_total)
+    near_here = summed(near_here, near_back)
+    f_total = summed(f_total, far_here[:rows]).astype(BF16)
+    b_total, f_total = join(backward(b_total), backward(f_total))
+    b_total = summed(b_total, b_parts[0], other_core(b_parts[4]), b0[2 * rows :]).astype(BF16)
+    f_total = summed(f_total, near_here[rows:]).astype(BF16)
+    b_total, f_total = join(b_total, f_total)
+    f_total = summed(backward(f_total), near_here[:rows], forward_in[0]).astype(BF16)
+    forward_next = to_home(f_total, 1, False)
+    backward_out = to_home(b_total[:rows], -1, False) + to_home(b_total[rows:], -1, True)
     return (forward_next[None], backward_out[None])
 
 

time: 158 us -> 156 us (0.987)
  waiting for transfers between devices: 73.9 us -> 94.2 us
  local copies, waits for them, and re-layouts: 19.7 us -> 1.77 us
  starting transfers between devices: 38.3 us -> 30.4 us
  Pallas kernels: 20 us -> 22.6 us
    ppermute x30 -> x34, waiting for transfers between devices: 65.1 us -> 85.5 us  [moved(): return lax.ppermute(block, 'expert', pairs)]
    unnamed x72 -> x13, local copies, waits for them, and re-layouts: 19.7 us -> 1.64 us
    ppermute x30 -> x34, starting transfers between devices: 29.2 us -> 22.2 us  [moved(): return lax.ppermute(block, 'expert', pairs)]
    pallas_call x2, Pallas kernels: 20 us -> 22.6 us  [expert_parts(): pl.pallas_call(body, grid=(2 * steps,), in_specs=[pl.BlockSpec((per_piece...]
    ppermute x4 -> x3, starting transfers between devices: 9.06 us -> 8.29 us  [to_home(): return lax.ppermute(block, ('pipe', 'expert'), pairs)]
    ppermute x4 -> x3, waiting for transfers between devices: 8.84 us -> 8.65 us  [to_home(): return lax.ppermute(block, ('pipe', 'expert'), pairs)]
  transfers between devices with their start and end apart: 34 -> 37, of which waited for: 18 -> 22; matrix products, arithmetic and copies ran while one was open for 2% -> 2% of each run, Pallas kernels for 13% -> 15%
where the time goes in v1:
time: 156 us
  waiting for transfers between devices  94.2 us (60%)
  starting transfers between devices  30.4 us (19%)
  Pallas kernels  22.6 us (14%)
  other arithmetic  5.78 us (4%)
  local copies, waits for them, and re-layouts  1.77 us (1%)
    ppermute x34, waiting for transfers between devices, moved(): return lax.ppermute(block, 'expert', pairs)  85.5 us
    pallas_call x2, Pallas kernels, expert_parts(): pl.pallas_call(body, grid=(2 * steps,), in_specs=[pl.BlockSpec((per_piece...  22.6 us
    ppermute x34, starting transfers between devices, moved(): return lax.ppermute(block, 'expert', pairs)  22.2 us
    ppermute x3, waiting for transfers between devices, to_home(): return lax.ppermute(block, ('pipe', 'expert'), pairs)  8.65 us
    ppermute x3, starting transfers between devices, to_home(): return lax.ppermute(block, ('pipe', 'expert'), pairs)  8.29 us
  transfers between devices with their start and end apart: 37, of which 22 were waited for; matrix products, arithmetic and copies ran while one was open for 2% of the time, Pallas kernels for 15%

profile of v1, /device:TPU:4, one launch (start us, length us, event | category | flops | bytes accessed | tf_op | source)
XLA Modules:
  0.0 155.6 jit_solution(5097725444979764571)
XLA Ops:
  6.7 9.3 %collective-permute-done = bf16[16,7168]{1,0:T(8,128)(2,1)S(1)} collective-permute-done((bf16[16,7168]{1,0:T(8,128)(2,1)S(1)}, bf16[16,7168]{1,0:T(8,128)(2,1)S(1)}, u32[]{:S(2)}, u32[]{:S(2)}) %collective-permute-start) | collective-permute-done | bytes 229408 | tf_op jit(solution)/shard_map/ppermute | solution.py:29
  16.5 8.5 %collective-permute-done.2 = bf16[16,7168]{1,0:T(8,128)(2,1)S(1)} collective-permute-done((bf16[16,7168]{1,0:T(8,128)(2,1)S(1)}, bf16[16,7168]{1,0:T(8,128)(2,1)S(1)}, u32[]{:S(2)}, u32[]{:S(2)}) %collective-permute-start.2) | collective-permute-done | bytes 229408 | tf_op jit(solution)/shard_map/ppermute | solution.py:29
  25.2 1.8 %collective-permute-start.5 = (bf16[32,7296]{1,0:T(8,128)(2,1)S(1)}, bf16[32,7296]{1,0:T(8,128)(2,1)S(1)}, u32[]{:S(2)}, u32[]{:S(2)}) collective-permute-start(bf16[32,7296]{1,0:T(8,128)(2,1)S(1)} %pad_maximum_fusion.1.refs_0_.refs_8_), channel_id=1, source_target_pairs={{0,8},{1,9},{2,10},{3,11},{4,12},{5,13},{6,14},{7,15},{8,0},{9,1},... | collective-permute-start | bytes 1400840 | tf_op jit(solution)/shard_map/ppermute | solution.py:29
  27.0 15.3 %collective-permute-done.6 = bf16[16,7296]{1,0:T(8,128)(2,1)S(1)} collective-permute-done((bf16[16,7296]{1,0:T(8,128)(2,1)S(1)}, bf16[16,7296]{1,0:T(8,128)(2,1)S(1)}, u32[]{:S(2)}, u32[]{:S(2)}) %collective-permute-start.6) | collective-permute-done | bytes 233504 | tf_op jit(solution)/shard_map/ppermute | solution.py:29
  42.5 1.8 %collective-permute-start.8 = (bf16[32,7296]{1,0:T(8,128)(2,1)S(1)}, bf16[32,7296]{1,0:T(8,128)(2,1)S(1)}, u32[]{:S(2)}, u32[]{:S(2)}) collective-permute-start(bf16[32,7296]{1,0:T(8,128)(2,1)S(1)} %pad_maximum_fusion.2.refs_1_.refs_9_), channel_id=1, source_target_pairs={{0,8},{1,9},{2,10},{3,11},{4,12},{5,13},{6,14},{7,15},{8,0},{9,1},... | collective-permute-start | bytes 1400840 | tf_op jit(solution)/shard_map/ppermute | solution.py:29
  44.7 10.0 %collective-permute-done.8.refs_3_.refs_11_ = bf16[32,7296]{1,0:T(8,128)(2,1)S(1)} collective-permute-done((bf16[32,7296]{1,0:T(8,128)(2,1)S(1)}, bf16[32,7296]{1,0:T(8,128)(2,1)S(1)}, u32[]{:S(2)}, u32[]{:S(2)}) %collective-permute-start.8) | collective-permute-done | bytes 466976 | tf_op jit(solution)/shard_map/ppermute | solution.py:29
  54.7 2.4 %collective-permute-done.7.refs_2_ = bf16[64,7168]{1,0:T(8,128)(2,1)S(1)} collective-permute-done((bf16[64,7168]{1,0:T(8,128)(2,1)S(1)}, bf16[64,7168]{1,0:T(8,128)(2,1)S(1)}, u32[]{:S(2)}, u32[]{:S(2)}) %collective-permute-start.7) | collective-permute-done | bytes 917536 | tf_op jit(solution)/shard_map/ppermute | solution.py:29
  58.0 1.9 %collective-permute-done.12.refs_7_.refs_15_ = bf16[32,7296]{1,0:T(8,128)(2,1)} collective-permute-done((bf16[32,7296]{1,0:T(8,128)(2,1)S(1)}, bf16[32,7296]{1,0:T(8,128)(2,1)}, u32[]{:S(2)}, u32[]{:S(2)}) %collective-permute-start.12) | collective-permute-done | bytes 466976 | tf_op jit(solution)/shard_map/ppermute | solution.py:29
  60.0 10.7 %shard_map.104 = (bf16[32,7168]{1,0:T(8,128)(2,1)S(1)}, bf16[32,7168]{1,0:T(8,128)(2,1)S(1)}, bf16[32,7168]{1,0:T(8,128)(2,1)S(1)}, bf16[32,7168]{1,0:T(8,128)(2...) custom-call(bf16[32,7296]{1,0:T(8,128)(2,1)S(1)} %pad_maximum_fusion, ...), custom_call_target="tpu_custom_call" | custom-call | flops 2818572288 | bytes 18350080 | tf_op jit(solution)/shard_map/pallas_call | solution.py:227
  70.7 4.1 %collective-permute-done.13.refs_3_ = bf16[64,7168]{1,0:T(8,128)(2,1)} collective-permute-done((bf16[64,7168]{1,0:T(8,128)(2,1)}, bf16[64,7168]{1,0:T(8,128)(2,1)}, u32[]{:S(2)}, u32[]{:S(2)}) %collective-permute-start.13) | collective-permute-done | bytes 917536 | tf_op jit(solution)/shard_map/ppermute | solution.py:29
  78.1 2.5 %collective-permute-done.16.refs_5_ = bf16[64,7168]{1,0:T(8,128)(2,1)S(1)} collective-permute-done((bf16[64,7168]{1,0:T(8,128)(2,1)S(1)}, bf16[64,7168]{1,0:T(8,128)(2,1)S(1)}, u32[]{:S(2)}, u32[]{:S(2)}) %collective-permute-start.16) | collective-permute-done | bytes 917536 | tf_op jit(solution)/shard_map/ppermute | solution.py:29
  81.9 1.7 %collective-permute-start.19 = (bf16[32,7168]{1,0:T(8,128)(2,1)S(1)}, bf16[32,7168]{1,0:T(8,128)(2,1)S(1)}, u32[]{:S(2)}, u32[]{:S(2)}) collective-permute-start(bf16[32,7168]{1,0:T(8,128)(2,1)S(1)} %add_convert_fusion.5), channel_id=1, source_target_pairs={{0,8},{1,9},{2,10},{3,11},{4,12},{5,13},{6,14},{7,15},{8,0},{9,1},... | collective-permute-start | bytes 1376264 | tf_op jit(solution)/shard_map/ppermute | solution.py:29
  83.7 11.9 %shard_map.105 = (bf16[32,7168]{1,0:T(8,128)(2,1)S(1)}, bf16[32,7168]{1,0:T(8,128)(2,1)S(1)}, bf16[32,7168]{1,0:T(8,128)(2,1)S(1)}, bf16[32,7168]{1,0:T(8,128)(2...) custom-call(bf16[64,7168]{1,0:T(8,128)(2,1)S(1)} %pad_maximum_fusion, ...), custom_call_target="tpu_custom_call" | custom-call | flops 4697620480 | bytes 25690112 | tf_op jit(solution)/shard_map/pallas_call | solution.py:227
  98.5 8.0 %collective-permute-done.23 = bf16[32,7168]{1,0:T(8,128)(2,1)S(1)} collective-permute-done((bf16[32,7168]{1,0:T(8,128)(2,1)S(1)}, bf16[32,7168]{1,0:T(8,128)(2,1)S(1)}, u32[]{:S(2)}, u32[]{:S(2)}) %collective-permute-start.23) | collective-permute-done | bytes 458784 | tf_op jit(solution)/shard_map/ppermute | solution.py:29
  109.9 1.7 %collective-permute-start.27 = (bf16[32,7168]{1,0:T(8,128)(2,1)S(1)}, bf16[32,7168]{1,0:T(8,128)(2,1)S(1)}, u32[]{:S(2)}, u32[]{:S(2)}) collective-permute-start(bf16[32,7168]{1,0:T(8,128)(2,1)S(1)} %add_convert_fusion.4), channel_id=1, source_target_pairs={{0,8},{1,9},{2,10},{3,11},{4,12},{5,13},{6,14},{7,15},{8,0},{9,1},... | collective-permute-start | bytes 1376264 | tf_op jit(solution)/shard_map/ppermute | solution.py:29
  111.6 3.6 %collective-permute-done.25 = bf16[32,7168]{1,0:T(8,128)(2,1)S(1)} collective-permute-done((bf16[32,7168]{1,0:T(8,128)(2,1)S(1)}, bf16[32,7168]{1,0:T(8,128)(2,1)S(1)}, u32[]{:S(2)}, u32[]{:S(2)}) %collective-permute-start.25) | collective-permute-done | bytes 458784 | tf_op jit(solution)/shard_map/ppermute | solution.py:29
  115.4 2.3 %collective-permute-done.28 = bf16[16,7168]{1,0:T(8,128)(2,1)S(1)} collective-permute-done((bf16[16,7168]{1,0:T(8,128)(2,1)S(1)}, bf16[16,7168]{1,0:T(8,128)(2,1)S(1)}, u32[]{:S(2)}, u32[]{:S(2)}) %collective-permute-start.28) | collective-permute-done | bytes 229408 | tf_op jit(solution)/shard_map/ppermute | solution.py:29
  117.7 5.3 %collective-permute-done.27 = bf16[32,7168]{1,0:T(8,128)(2,1)S(1)} collective-permute-done((bf16[32,7168]{1,0:T(8,128)(2,1)S(1)}, bf16[32,7168]{1,0:T(8,128)(2,1)S(1)}, u32[]{:S(2)}, u32[]{:S(2)}) %collective-permute-start.27) | collective-permute-done | bytes 458784 | tf_op jit(solution)/shard_map/ppermute | solution.py:29
  126.4 2.7 %collective-permute-done.30 = bf16[16,7168]{1,0:T(8,128)(2,1)S(1)} collective-permute-done((bf16[16,7168]{1,0:T(8,128)(2,1)S(1)}, bf16[16,7168]{1,0:T(8,128)(2,1)S(1)}, u32[]{:S(2)}, u32[]{:S(2)}) %collective-permute-start.30) | collective-permute-done | bytes 229408 | tf_op jit(solution)/shard_map/ppermute | solution.py:29
  129.1 4.9 %collective-permute-done.29 = bf16[32,7168]{1,0:T(8,128)(2,1)S(1)} collective-permute-done((bf16[32,7168]{1,0:T(8,128)(2,1)S(1)}, bf16[32,7168]{1,0:T(8,128)(2,1)S(1)}, u32[]{:S(2)}, u32[]{:S(2)}) %collective-permute-start.29) | collective-permute-done | bytes 458784 | tf_op jit(solution)/shard_map/ppermute | solution.py:29
  134.3 2.9 %collective-permute-start.33 = (bf16[16,7168]{1,0:T(8,128)(2,1)S(1)}, bf16[16,7168]{1,0:T(8,128)(2,1)S(1)}, u32[]{:S(2)}, u32[]{:S(2)}) collective-permute-start(bf16[16,7168]{1,0:T(8,128)(2,1)S(1)} %fusion.2), channel_id=1, source_target_pairs={{0,6},{1,3},{2,0},{3,5},{4,2},{5,7},{6,4},{7,1},{8,14},{9,11},{10,... | collective-permute-start | bytes 688136 | tf_op jit(solution)/shard_map/ppermute | solution.py:29
  137.2 6.2 %collective-permute-start.36 = (bf16[16,7168]{1,0:T(8,128)(2,1)S(1)}, bf16[16,7168]{1,0:T(8,128)(2,1)S(1)}, u32[]{:S(2)}, u32[]{:S(2)}) collective-permute-start(bf16[16,7168]{1,0:T(8,128)(2,1)S(1)} %get-tuple-element.160), channel_id=1, source_target_pairs={{0,248},{1,249},{2,250},{3,251},{4,252},{5,253},{6,254},{7,255},{8... | collective-permute-start | bytes 688136 | tf_op jit(solution)/shard_map/ppermute | solution.py:68
  143.3 2.0 %collective-permute-start.35 = (bf16[16,7168]{1,0:T(8,128)(2,1)S(1)}, bf16[16,7168]{1,0:T(8,128)(2,1)S(1)}, u32[]{:S(2)}, u32[]{:S(2)}) collective-permute-start(bf16[16,7168]{1,0:T(8,128)(2,1)S(1)} %get-tuple-element.161), channel_id=1, source_target_pairs={{0,240},{1,241},{2,242},{3,243},{4,244},{5,245},{6,246},{7,247},{8... | collective-permute-start | bytes 688136 | tf_op jit(solution)/shard_map/ppermute | solution.py:68
  147.0 7.2 %collective-permute-done.35 = bf16[16,7168]{1,0:T(8,128)(2,1)S(1)} collective-permute-done((bf16[16,7168]{1,0:T(8,128)(2,1)S(1)}, bf16[16,7168]{1,0:T(8,128)(2,1)S(1)}, u32[]{:S(2)}, u32[]{:S(2)}) %collective-permute-start.35) | collective-permute-done | bytes 229408 | tf_op jit(solution)/shard_map/ppermute | solution.py:68
  (89 shorter events, 26.2 us)
Async XLA Ops:
  2.4 13.5 %collective-permute-start.1 = (bf16[16,7296]{1,0:T(8,128)(2,1)S(1)}, bf16[16,7296]{1,0:T(8,128)(2,1)S(1)}, u32[]{:S(2)}, u32[]{:S(2)}) collective-permute-start(bf16[16,7296]{1,0:T(8,128)(2,1)S(1)} %pad_maximum_fusion.3), channel_id=1, source_target_pairs={{0,2},{1,7},{2,4},{3,1},{4,6},{5,3},{6,0},{7,5},{8,10},{9,15},{10,... | collective-permute-start | bytes 700424 | tf_op jit(solution)/shard_map/ppermute | solution.py:29
  5.9 10.0 %collective-permute-start = (bf16[16,7168]{1,0:T(8,128)(2,1)S(1)}, bf16[16,7168]{1,0:T(8,128)(2,1)S(1)}, u32[]{:S(2)}, u32[]{:S(2)}) collective-permute-start(bf16[16,7168]{1,0:T(8,128)(2,1)S(1)} %get-tuple-element.163), channel_id=1, source_target_pairs={{0,8},{1,9},{2,10},{3,11},{4,12},{5,13},{6,14},{7,15},{8,0},{9,1},... | collective-permute-start | bytes 688136 | tf_op jit(solution)/shard_map/ppermute | solution.py:29
  15.9 9.1 %collective-permute-start.2 = (bf16[16,7168]{1,0:T(8,128)(2,1)S(1)}, bf16[16,7168]{1,0:T(8,128)(2,1)S(1)}, u32[]{:S(2)}, u32[]{:S(2)}) collective-permute-start(bf16[16,7168]{1,0:T(8,128)(2,1)S(1)} %get-tuple-element.83), channel_id=1, source_target_pairs={{0,8},{1,9},{2,10},{3,11},{4,12},{5,13},{6,14},{7,15},{8,0},{9,1},... | collective-permute-start | bytes 688136 | tf_op jit(solution)/shard_map/ppermute | solution.py:29
  25.1 17.2 %collective-permute-start.4 = (bf16[64,7168]{1,0:T(8,128)(2,1)S(1)}, bf16[64,7168]{1,0:T(8,128)(2,1)S(1)}, u32[]{:S(2)}, u32[]{:S(2)}) collective-permute-start(bf16[64,7168]{1,0:T(8,128)(2,1)S(1)} %pad_maximum_fusion.refs_0_), channel_id=1, source_target_pairs={{0,2},{1,7},{2,4},{3,1},{4,6},{5,3},{6,0},{7,5},{8,10},{9,15},{10,... | collective-permute-start | bytes 2752520 | tf_op jit(solution)/shard_map/ppermute | solution.py:29
  25.2 17.1 %collective-permute-start.5 = (bf16[32,7296]{1,0:T(8,128)(2,1)S(1)}, bf16[32,7296]{1,0:T(8,128)(2,1)S(1)}, u32[]{:S(2)}, u32[]{:S(2)}) collective-permute-start(bf16[32,7296]{1,0:T(8,128)(2,1)S(1)} %pad_maximum_fusion.1.refs_0_.refs_8_), channel_id=1, source_target_pairs={{0,8},{1,9},{2,10},{3,11},{4,12},{5,13},{6,14},{7,15},{8,0},{9,1},... | collective-permute-start | bytes 1400840 | tf_op jit(solution)/shard_map/ppermute | solution.py:29
  27.0 15.3 %collective-permute-start.6 = (bf16[16,7296]{1,0:T(8,128)(2,1)S(1)}, bf16[16,7296]{1,0:T(8,128)(2,1)S(1)}, u32[]{:S(2)}, u32[]{:S(2)}) collective-permute-start(bf16[16,7296]{1,0:T(8,128)(2,1)S(1)} %collective-permute-done.3), channel_id=1, source_target_pairs={{0,2},{1,7},{2,4},{3,1},{4,6},{5,3},{6,0},{7,5},{8,10},{9,15},{10,... | collective-permute-start | bytes 700424 | tf_op jit(solution)/shard_map/ppermute | solution.py:29
  42.4 14.7 %collective-permute-start.7 = (bf16[64,7168]{1,0:T(8,128)(2,1)S(1)}, bf16[64,7168]{1,0:T(8,128)(2,1)S(1)}, u32[]{:S(2)}, u32[]{:S(2)}) collective-permute-start(bf16[64,7168]{1,0:T(8,128)(2,1)S(1)} %collective-permute-done.4.refs_1_), channel_id=1, source_target_pairs={{0,2},{1,7},{2,4},{3,1},{4,6},{5,3},{6,0},{7,5},{8,10},{9,15},{10,... | collective-permute-start | bytes 2752520 | tf_op jit(solution)/shard_map/ppermute | solution.py:29
  42.5 12.2 %collective-permute-start.8 = (bf16[32,7296]{1,0:T(8,128)(2,1)S(1)}, bf16[32,7296]{1,0:T(8,128)(2,1)S(1)}, u32[]{:S(2)}, u32[]{:S(2)}) collective-permute-start(bf16[32,7296]{1,0:T(8,128)(2,1)S(1)} %pad_maximum_fusion.2.refs_1_.refs_9_), channel_id=1, source_target_pairs={{0,8},{1,9},{2,10},{3,11},{4,12},{5,13},{6,14},{7,15},{8,0},{9,1},... | collective-permute-start | bytes 1400840 | tf_op jit(solution)/shard_map/ppermute | solution.py:29
  44.2 13.8 %collective-permute-start.9 = (bf16[32,7296]{1,0:T(8,128)(2,1)S(1)}, bf16[32,7296]{1,0:T(8,128)(2,1)S(1)}, u32[]{:S(2)}, u32[]{:S(2)}) collective-permute-start(bf16[32,7296]{1,0:T(8,128)(2,1)S(1)} %pad_maximum_fusion.1.refs_0_.refs_8_), channel_id=1, source_target_pairs={{0,1},{1,0},{2,3},{3,2},{4,5},{5,4},{6,7},{7,6},{8,9},{9,8},{10,11... | collective-permute-start | bytes 1400840 | tf_op jit(solution)/shard_map/ppermute | solution.py:29
  44.2 13.8 %collective-permute-start.10 = (bf16[32,7296]{1,0:T(8,128)(2,1)S(1)}, bf16[32,7296]{1,0:T(8,128)(2,1)}, u32[]{:S(2)}, u32[]{:S(2)}) collective-permute-start(bf16[32,7296]{1,0:T(8,128)(2,1)S(1)} %pad_maximum_fusion.2.refs_1_.refs_9_), channel_id=1, source_target_pairs={{0,1},{1,0},{2,3},{3,2},{4,5},{5,4},{6,7},{7,6},{8,9},{9,8},{10,11... | collective-permute-start | bytes 1400840 | tf_op jit(solution)/shard_map/ppermute | solution.py:29
  44.7 13.3 %collective-permute-start.11 = (bf16[32,7296]{1,0:T(8,128)(2,1)S(1)}, bf16[32,7296]{1,0:T(8,128)(2,1)}, u32[]{:S(2)}, u32[]{:S(2)}) collective-permute-start(bf16[32,7296]{1,0:T(8,128)(2,1)S(1)} %collective-permute-done.5.refs_2_.refs_10_), channel_id=1, source_target_pairs={{0,1},{1,0},{2,3},{3,2},{4,5},{5,4},{6,7},{7,6},{8,9},{9,8},{10,11... | collective-permute-start | bytes 1400840 | tf_op jit(solution)/shard_map/ppermute | solution.py:29
  59.9 14.9 %collective-permute-start.13 = (bf16[64,7168]{1,0:T(8,128)(2,1)}, bf16[64,7168]{1,0:T(8,128)(2,1)}, u32[]{:S(2)}, u32[]{:S(2)}) collective-permute-start(bf16[64,7168]{1,0:T(8,128)(2,1)} %copy-done.2), channel_id=1, source_target_pairs={{0,2},{1,7},{2,4},{3,1},{4,6},{5,3},{6,0},{7,5},{8,10},{9,15},{10,... | collective-permute-start | bytes 2752520 | tf_op jit(solution)/shard_map/ppermute | solution.py:29
  78.0 18.0 %collective-permute-start.22 = (bf16[32,7168]{1,0:T(8,128)(2,1)S(1)}, bf16[32,7168]{1,0:T(8,128)(2,1)S(1)}, u32[]{:S(2)}, u32[]{:S(2)}) collective-permute-start(bf16[32,7168]{1,0:T(8,128)(2,1)S(1)} %get-tuple-element.140), channel_id=1, source_target_pairs={{0,1},{1,0},{2,3},{3,2},{4,5},{5,4},{6,7},{7,6},{8,9},{9,8},{10,11... | collective-permute-start | bytes 1376264 | tf_op jit(solution)/shard_map/ppermute | solution.py:29
  81.9 14.1 %collective-permute-start.19 = (bf16[32,7168]{1,0:T(8,128)(2,1)S(1)}, bf16[32,7168]{1,0:T(8,128)(2,1)S(1)}, u32[]{:S(2)}, u32[]{:S(2)}) collective-permute-start(bf16[32,7168]{1,0:T(8,128)(2,1)S(1)} %add_convert_fusion.5), channel_id=1, source_target_pairs={{0,8},{1,9},{2,10},{3,11},{4,12},{5,13},{6,14},{7,15},{8,0},{9,1},... | collective-permute-start | bytes 1376264 | tf_op jit(solution)/shard_map/ppermute | solution.py:29
  98.0 11.9 %collective-permute-start.26 = (bf16[32,7168]{1,0:T(8,128)(2,1)S(1)}, bf16[32,7168]{1,0:T(8,128)(2,1)S(1)}, u32[]{:S(2)}, u32[]{:S(2)}) collective-permute-start(bf16[32,7168]{1,0:T(8,128)(2,1)S(1)} %get-tuple-element.146), channel_id=1, source_target_pairs={{0,1},{1,0},{2,3},{3,2},{4,5},{5,4},{6,7},{7,6},{8,9},{9,8},{10,11... | collective-permute-start | bytes 1376264 | tf_op jit(solution)/shard_map/ppermute | solution.py:29
  108.0 18.3 %collective-permute-start.32 = (bf16[32,7168]{1,0:T(8,128)(2,1)S(1)}, bf16[32,7168]{1,0:T(8,128)(2,1)S(1)}, u32[]{:S(2)}, u32[]{:S(2)}) collective-permute-start(bf16[32,7168]{1,0:T(8,128)(2,1)S(1)} %get-tuple-element.156), channel_id=1, source_target_pairs={{0,1},{1,0},{2,3},{3,2},{4,5},{5,4},{6,7},{7,6},{8,9},{9,8},{10,11... | collective-permute-start | bytes 1376264 | tf_op jit(solution)/shard_map/ppermute | solution.py:29
  108.0 26.1 %collective-permute-start.31 = (bf16[32,7168]{1,0:T(8,128)(2,1)S(1)}, bf16[32,7168]{1,0:T(8,128)(2,1)S(1)}, u32[]{:S(2)}, u32[]{:S(2)}) collective-permute-start(bf16[32,7168]{1,0:T(8,128)(2,1)S(1)} %get-tuple-element.153), channel_id=1, source_target_pairs={{0,1},{1,0},{2,3},{3,2},{4,5},{5,4},{6,7},{7,6},{8,9},{9,8},{10,11... | collective-permute-start | bytes 1376264 | tf_op jit(solution)/shard_map/ppermute | solution.py:29
  108.5 9.2 %collective-permute-start.28 = (bf16[16,7168]{1,0:T(8,128)(2,1)S(1)}, bf16[16,7168]{1,0:T(8,128)(2,1)S(1)}, u32[]{:S(2)}, u32[]{:S(2)}) collective-permute-start(bf16[16,7168]{1,0:T(8,128)(2,1)S(1)} %slice.58), channel_id=1, source_target_pairs={{0,6},{1,3},{2,0},{3,5},{4,2},{5,7},{6,4},{7,1},{8,14},{9,11},{10,... | collective-permute-start | bytes 688136 | tf_op jit(solution)/shard_map/ppermute | solution.py:29
  109.9 13.0 %collective-permute-start.27 = (bf16[32,7168]{1,0:T(8,128)(2,1)S(1)}, bf16[32,7168]{1,0:T(8,128)(2,1)S(1)}, u32[]{:S(2)}, u32[]{:S(2)}) collective-permute-start(bf16[32,7168]{1,0:T(8,128)(2,1)S(1)} %add_convert_fusion.4), channel_id=1, source_target_pairs={{0,8},{1,9},{2,10},{3,11},{4,12},{5,13},{6,14},{7,15},{8,0},{9,1},... | collective-permute-start | bytes 1376264 | tf_op jit(solution)/shard_map/ppermute | solution.py:29
  124.6 9.4 %collective-permute-start.29 = (bf16[32,7168]{1,0:T(8,128)(2,1)S(1)}, bf16[32,7168]{1,0:T(8,128)(2,1)S(1)}, u32[]{:S(2)}, u32[]{:S(2)}) collective-permute-start(bf16[32,7168]{1,0:T(8,128)(2,1)S(1)} %add_convert_fusion.1), channel_id=1, source_target_pairs={{0,6},{1,3},{2,0},{3,5},{4,2},{5,7},{6,4},{7,1},{8,14},{9,11},{10,... | collective-permute-start | bytes 1376264 | tf_op jit(solution)/shard_map/ppermute | solution.py:29
  134.3 11.1 %collective-permute-start.33 = (bf16[16,7168]{1,0:T(8,128)(2,1)S(1)}, bf16[16,7168]{1,0:T(8,128)(2,1)S(1)}, u32[]{:S(2)}, u32[]{:S(2)}) collective-permute-start(bf16[16,7168]{1,0:T(8,128)(2,1)S(1)} %fusion.2), channel_id=1, source_target_pairs={{0,6},{1,3},{2,0},{3,5},{4,2},{5,7},{6,4},{7,1},{8,14},{9,11},{10,... | collective-permute-start | bytes 688136 | tf_op jit(solution)/shard_map/ppermute | solution.py:29
  137.2 9.8 %collective-permute-start.36 = (bf16[16,7168]{1,0:T(8,128)(2,1)S(1)}, bf16[16,7168]{1,0:T(8,128)(2,1)S(1)}, u32[]{:S(2)}, u32[]{:S(2)}) collective-permute-start(bf16[16,7168]{1,0:T(8,128)(2,1)S(1)} %get-tuple-element.160), channel_id=1, source_target_pairs={{0,248},{1,249},{2,250},{3,251},{4,252},{5,253},{6,254},{7,255},{8... | collective-permute-start | bytes 688136 | tf_op jit(solution)/shard_map/ppermute | solution.py:68
  143.3 10.9 %collective-permute-start.35 = (bf16[16,7168]{1,0:T(8,128)(2,1)S(1)}, bf16[16,7168]{1,0:T(8,128)(2,1)S(1)}, u32[]{:S(2)}, u32[]{:S(2)}) collective-permute-start(bf16[16,7168]{1,0:T(8,128)(2,1)S(1)} %get-tuple-element.161), channel_id=1, source_target_pairs={{0,240},{1,241},{2,242},{3,243},{4,244},{5,245},{6,246},{7,247},{8... | collective-permute-start | bytes 688136 | tf_op jit(solution)/shard_map/ppermute | solution.py:68
  145.5 9.5 %collective-permute-start.34 = (bf16[16,7168]{1,0:T(8,128)(2,1)S(1)}, bf16[16,7168]{1,0:T(8,128)(2,1)S(1)}, u32[]{:S(2)}, u32[]{:S(2)}) collective-permute-start(bf16[16,7168]{1,0:T(8,128)(2,1)S(1)} %fusion.1), channel_id=1, source_target_pairs={{0,16},{1,17},{2,18},{3,19},{4,20},{5,21},{6,22},{7,23},{8,24},{9,... | collective-permute-start | bytes 688136 | tf_op jit(solution)/shard_map/ppermute | solution.py:68
  (19 other events, 171.4 us)

commit v2 on v1

--- a/solution.py
+++ b/solution.py
@@ -47,6 +47,14 @@
 
 def backward(block):
     return moved(block, lambda column, chip, core: (column, chip - 1 + 2 * core, core))
+
+
+def opposite(block):
+    return moved(block, lambda column, chip, core: (column, chip + 2, core))
+
+
+def after(block, *others):
+    return lax.optimization_barrier((block, *others))[0]
 
 
 def to_home(block, distance, cross):
@@ -95,11 +103,19 @@
     return 1.0 / (1.0 + jnp.exp(-values))
 
 
+def store(part, out_refs):
+    start = 0
+    for ref in out_refs:
+        rows = ref.shape[0]
+        ref[...] = part[start : start + rows]
+        start += rows
+
+
 def forward_kernel(count, steps, *refs):
     x_refs, route_refs = refs[:count], refs[count : 2 * count]
     gate_ref, up_ref, down_ref, router_ref, column_ref = refs[2 * count : 2 * count + 5]
-    out_refs = refs[2 * count + 5 : 3 * count + 5]
-    gate_acc, up_acc, logit_acc, hidden, gates = refs[3 * count + 5 :]
+    out_refs = refs[2 * count + 5 : -5]
+    gate_acc, up_acc, logit_acc, hidden, gates = refs[-5:]
     i = pl.program_id(0)
 
     @pl.when(i == 0)
@@ -127,16 +143,14 @@
     @pl.when(i >= steps)
     def _():
         part = (gates[...] * dot(hidden[...], down_ref[...])).astype(BF16)
-        rows = part.shape[0] // count
-        for j, ref in enumerate(out_refs):
-            ref[...] = part[j * rows : (j + 1) * rows]
+        store(part, out_refs)
 
 
 def backward_kernel(count, steps, *refs):
-    x_refs = refs[:count]
-    gate_ref, up_ref, down_ref, router_ref = refs[count : count + 4]
-    out_refs = refs[count + 4 : 2 * count + 4]
-    gate_acc, up_acc, down_acc, logit_acc, gate_slope, up_slope, weight = refs[2 * count + 4 :]
+    x_refs, grad_refs = refs[:count], refs[count : 2 * count]
+    gate_ref, up_ref, down_ref, router_ref = refs[2 * count : 2 * count + 4]
+    out_refs = refs[2 * count + 4 : -7]
+    gate_acc, up_acc, down_acc, logit_acc, gate_slope, up_slope, weight = refs[-7:]
     i = pl.program_id(0)
 
     @pl.when(i == 0)
@@ -148,9 +162,8 @@
 
     @pl.when(i < steps)
     def _():
-        rows = x_refs[0].shape[0] // 2
-        x = jnp.concatenate([ref[:rows] for ref in x_refs], axis=0)
-        grad = jnp.concatenate([ref[rows:] for ref in x_refs], axis=0)
+        x = jnp.concatenate([ref[...] for ref in x_refs], axis=0)
+        grad = jnp.concatenate([ref[...] for ref in grad_refs], axis=0)
         gate_acc[...] += dot(x, gate_ref[...])
         up_acc[...] += dot(x, up_ref[...])
         down_acc[...] += dot_turned(grad, down_ref[...])
@@ -175,18 +188,16 @@
         through = dot_turned(gate_slope[...], gate_ref[...])
         through += dot_turned(up_slope[...], up_ref[...])
         part = (through + weight[...] * router_ref[...]).astype(BF16)
-        rows = part.shape[0] // count
-        for j, ref in enumerate(out_refs):
-            ref[...] = part[j * rows : (j + 1) * rows]
-
-
-def expert_parts(pieces, gate, up, down, router_row, column_row, is_backward):
+        store(part, out_refs)
+
+
+def expert_parts(pieces, grads, out_rows, gate, up, down, router_row, column_row):
+    is_backward = grads is not None
     model, hidden_units = gate.shape
     steps = model // TILE
     count = len(pieces)
     per_piece = pieces[0].shape[0]
-    token_rows = per_piece // 2 if is_backward else per_piece
-    rows = token_rows * count
+    rows = per_piece * count
 
     def first(i):
         return jnp.minimum(i, steps - 1)
@@ -220,6 +231,7 @@
             pltpu.VMEM((rows, 1), F32),
         ]
     products = 5 if is_backward else 3
+    x_specs = [pl.BlockSpec((per_piece, TILE), lambda i: (0, first(i)))] * count
     route_specs = [pl.BlockSpec((per_piece, LANES), lambda i: (0, model // LANES))] * count
     gate, up, down = (
         pltpu.with_memory_space_constraint(weight, pltpu.HBM) for weight in (gate, up, down)
@@ -227,8 +239,7 @@
     return pl.pallas_call(
         body,
         grid=(2 * steps,),
-        in_specs=[pl.BlockSpec((per_piece, TILE), lambda i: (0, first(i)))] * count
-        + ([] if is_backward else route_specs)
+        in_specs=x_specs + (x_specs if is_backward else route_specs)
         + [
             pl.BlockSpec((TILE, hidden_units), lambda i: (weight_at(i), 0)),
             pl.BlockSpec((TILE, hidden_units), lambda i: (weight_at(i), 0)),
@@ -236,8 +247,8 @@
             pl.BlockSpec((1, TILE), lambda i: (0, router_at(i))),
         ]
         + ([] if is_backward else [pl.BlockSpec((1, LANES), lambda i: (0, 0))]),
-        out_specs=[pl.BlockSpec((token_rows, TILE), lambda i: (0, second(i)))] * count,
-        out_shape=[jax.ShapeDtypeStruct((token_rows, model), BF16)] * count,
+        out_specs=[pl.BlockSpec((n, TILE), lambda i: (0, second(i))) for n in out_rows],
+        out_shape=[jax.ShapeDtypeStruct((n, model), BF16) for n in out_rows],
         scratch_shapes=scratch,
         compiler_params=pltpu.CompilerParams(vmem_limit_bytes=24 * 1024 * 1024),
         cost_estimate=pl.CostEstimate(
@@ -247,7 +258,7 @@
         ),
     )(
         *pieces,
-        *([] if is_backward else pieces),
+        *(grads if is_backward else pieces),
         gate,
         up,
         down,
@@ -287,50 +298,68 @@
     lanes = jnp.broadcast_to(forward_route[0].astype(BF16)[:, None], (rows, LANES))
     f0 = jnp.concatenate([forward_in[0], lanes], axis=1)
 
-    x_arrived, f1 = join(other_column(x_cross), onward(f0))
-    f1, grad_cross = join(f1, grad_cross)
-    grad_arrived, f2 = join(other_column(grad_cross), onward(f1))
-    b0 = stack(x_own, x_arrived, grad_own, grad_arrived)
-    near = stack(f0, f1)
-    b0, near, f2 = join(b0, near, f2)
-    b1, near_crossed, f3 = join(onward(b0), other_column(near), onward(f2))
-    far = stack(f2, f3)
-    b1, far = join(b1, far)
-    b2, far_crossed = join(onward(b1), other_column(far))
-    pieces = [near, far, near_crossed, far_crossed]
-    pieces = pieces + [other_core(piece) for piece in pieces]
-    b2, *pieces = join(b2, *pieces)
-    parts = expert_parts(pieces, *weights, router_row, column_row, False)
-    b3, *parts = join(onward(b2), *parts)
-
-    far_back = summed(parts[3], other_core(parts[7])).astype(BF16)
-    pieces = [b0, b1, b2, b3]
-    pieces = pieces + [other_core(piece) for piece in pieces]
-    far_back, *pieces = join(far_back, *pieces)
-    near_back = summed(parts[2], other_core(parts[6])).astype(BF16)
-    far_here = summed(parts[1], other_core(parts[5]))
-    near_here = summed(parts[0], other_core(parts[4]))
-    b_parts = expert_parts(pieces, *weights, router_row, column_row, True)
-    far_back, near_back, *b_parts = join(other_column(far_back), near_back, *b_parts)
-
-    far_here = summed(far_here, far_back)
-    b_total = summed(b_parts[3], other_core(b_parts[7])).astype(BF16)
-    f_total = far_here[rows:].astype(BF16)
-    near_back, b_total, f_total = join(near_back, b_total, f_total)
-    near_back, f_total = other_column(near_back), backward(f_total)
-    b_total = summed(backward(b_total), b_parts[2], other_core(b_parts[6])).astype(BF16)
-    b_total = summed(backward(b_total), b_parts[1], other_core(b_parts[5])).astype(BF16)
-    b_total, near_back, f_total = join(b_total, near_back, f_total)
-    near_here = summed(near_here, near_back)
-    f_total = summed(f_total, far_here[:rows]).astype(BF16)
-    b_total, f_total = join(backward(b_total), backward(f_total))
-    b_total = summed(b_total, b_parts[0], other_core(b_parts[4]), b0[2 * rows :]).astype(BF16)
-    f_total = summed(f_total, near_here[rows:]).astype(BF16)
-    b_total, f_total = join(b_total, f_total)
-    f_total = summed(backward(f_total), near_here[:rows], forward_in[0]).astype(BF16)
+    x_arrived = other_column(x_cross)
+    f1, f3, f2 = onward(f0), backward(f0), opposite(f0)
+    grad_arrived = other_column(grad_cross)
+    x0 = stack(x_own, x_arrived)
+    x1 = onward(x0)
+    here = stack(f0, f1, f2, f3)
+    crossed = other_column(after(here, x0))
+    g0 = stack(grad_own, after(grad_arrived, here))
+    g1 = onward(g0)
+    x2 = onward(after(x1, g0))
+    g2 = onward(after(g1, x1))
+    x3_from = after(x2, g1)
+    x3 = onward(x3_from)
+    g3_from = after(g2, x2)
+    g3 = onward(g3_from)
+    pieces = [here, crossed, other_core(here), other_core(crossed)]
+    pieces[-1] = after(pieces[-1], x3_from, g3_from)
+    parts = expert_parts(pieces, None, [4 * rows] * 4, *weights, router_row, column_row)
+    x3, g3, *parts = join(x3, g3, *parts)
+
+    cross_sum = summed(parts[1], other_core(parts[3])).astype(BF16)
+    far_back = cross_sum[2 * rows :]
+    xs, gs = [x0, x1, x2, x3], [g0, g1, g2, g3]
+    xs = xs + [other_core(x) for x in xs]
+    gs = gs + [other_core(g) for g in gs]
+    far_back, xs[-1], gs[-1] = join(far_back, xs[-1], gs[-1])
+    b_parts = expert_parts(
+        xs, gs, [rows] * 8 + [4 * rows] * 2, *weights, router_row, column_row
+    )
+    far_back, near_back, *b_parts = join(other_column(far_back), cross_sum[: 2 * rows], *b_parts)
+
+    b_other = [other_core(b_parts[9]), other_core(b_parts[8])]
+
+    def of_piece(j, cross):
+        start = ((j % 2) * 2 + cross) * rows
+        return b_parts[2 * j + cross], b_other[0 if j >= 2 else 1][start : start + rows]
+
+    own3 = summed(*of_piece(3, 0)).astype(BF16)
+    cross3 = summed(*of_piece(3, 1)).astype(BF16)
+    own3, cross3, near_back = join(own3, cross3, near_back)
+    own2, cross2, near_back = backward(own3), backward(cross3), other_column(near_back)
+    own2 = summed(own2, *of_piece(2, 0)).astype(BF16)
+    cross2 = summed(after(cross2, own2), *of_piece(2, 1)).astype(BF16)
+    own1, cross1 = backward(own2), backward(cross2)
+    near_back = after(near_back, cross2)
+    f_sum = summed(parts[0], other_core(parts[2]), stack(near_back, far_back))
+    f_send = f_sum.astype(BF16)
+    f_back = [
+        backward(f_send[rows : 2 * rows]),
+        opposite(f_send[2 * rows : 3 * rows]),
+        onward(f_send[3 * rows :]),
+    ]
+    own1 = summed(after(own1, f_send), *of_piece(1, 0)).astype(BF16)
+    cross1 = summed(after(cross1, own1), *of_piece(1, 1)).astype(BF16)
+    own0, cross0 = backward(own1), backward(cross1)
+    f_total = summed(f_sum[:rows], after(forward_in[0], cross1), *f_back).astype(BF16)
+    own0 = summed(after(own0, f_total), *of_piece(0, 0), grad_own).astype(BF16)
+    cross0 = summed(after(cross0, own0), *of_piece(0, 1), g0[rows:]).astype(BF16)
     forward_next = to_home(f_total, 1, False)
-    backward_out = to_home(b_total[:rows], -1, False) + to_home(b_total[rows:], -1, True)
-    return (forward_next[None], backward_out[None])
+    own_home = to_home(own0, -1, False)
+    cross_home = to_home(cross0, -1, True)
+    return (forward_next[None], (own_home + cross_home)[None])
 
 
 def solution(mesh):

time: 156 us -> 134 us (0.86)
  the two profiles are of different devices: /device:TPU:4 before, /device:TPU:1 now
where the time goes in v2:
time: 134 us; the launch traced here: 133 us
  starting transfers between devices  52 us (39%)
  waiting for transfers between devices  51.6 us (39%)
  Pallas kernels  22.1 us (16%)
  other arithmetic  5.78 us (4%)
    ppermute x37, waiting for transfers between devices, moved(): return lax.ppermute(block, 'expert', pairs)  45.5 us
    ppermute x37, starting transfers between devices, moved(): return lax.ppermute(block, 'expert', pairs)  42.8 us
    pallas_call x2, Pallas kernels, expert_parts(): pl.pallas_call(body, grid=(2 * steps,), in_specs=x_specs + (x_specs if is...  22.1 us
    ppermute x3, starting transfers between devices, to_home(): return lax.ppermute(block, ('pipe', 'expert'), pairs)  9.24 us
    ppermute x3, waiting for transfers between devices, to_home(): return lax.ppermute(block, ('pipe', 'expert'), pairs)  6.09 us
  transfers between devices with their start and end apart: 40, of which 23 were waited for; matrix products, arithmetic and copies ran while one was open for 2% of the time, Pallas kernels for 17%

profile of v2, /device:TPU:1, one launch (start us, length us, event | category | flops | bytes accessed | tf_op | source)
XLA Modules:
  0.0 133.3 jit_solution(15692664304276257886)
XLA Ops:
  2.6 3.7 %collective-permute-start = (bf16[16,7168]{1,0:T(8,128)(2,1)S(1)}, bf16[16,7168]{1,0:T(8,128)(2,1)S(1)}, u32[]{:S(2)}, u32[]{:S(2)}) collective-permute-start(bf16[16,7168]{1,0:T(8,128)(2,1)S(1)} %get-tuple-element.119), channel_id=1, source_target_pairs={{0,8},{1,9},{2,10},{3,11},{4,12},{5,13},{6,14},{7,15},{8,0},{9,1},... | collective-permute-start | bytes 688136 | tf_op jit(solution)/shard_map/ppermute | solution.py:29
  9.3 2.6 %collective-permute-start.4 = (bf16[16,7296]{1,0:T(8,128)(2,1)S(1)}, bf16[16,7296]{1,0:T(8,128)(2,1)S(1)}, u32[]{:S(2)}, u32[]{:S(2)}) collective-permute-start(bf16[16,7296]{1,0:T(8,128)(2,1)S(1)} %pad_maximum_fusion.3), channel_id=1, source_target_pairs={{0,4},{1,5},{2,6},{3,7},{4,0},{5,1},{6,2},{7,3},{8,12},{9,13},{10,... | collective-permute-start | bytes 700424 | tf_op jit(solution)/shard_map/ppermute | solution.py:29
  14.3 5.3 %collective-permute-done.4 = bf16[16,7296]{1,0:T(8,128)(2,1)S(1)} collective-permute-done((bf16[16,7296]{1,0:T(8,128)(2,1)S(1)}, bf16[16,7296]{1,0:T(8,128)(2,1)S(1)}, u32[]{:S(2)}, u32[]{:S(2)}) %collective-permute-start.4) | collective-permute-done | bytes 233504 | tf_op jit(solution)/shard_map/ppermute | solution.py:29
  19.6 2.5 %collective-permute-done.3 = bf16[16,7296]{1,0:T(8,128)(2,1)S(1)} collective-permute-done((bf16[16,7296]{1,0:T(8,128)(2,1)S(1)}, bf16[16,7296]{1,0:T(8,128)(2,1)S(1)}, u32[]{:S(2)}, u32[]{:S(2)}) %collective-permute-start.3) | collective-permute-done | bytes 233504 | tf_op jit(solution)/shard_map/ppermute | solution.py:29
  22.4 3.2 %collective-permute-start.7 = (bf16[32,7168]{1,0:T(8,128)(2,1)S(1)}, bf16[32,7168]{1,0:T(8,128)(2,1)}, u32[]{:S(2)}, u32[]{:S(2)}) collective-permute-start(bf16[32,7168]{1,0:T(8,128)(2,1)S(1)} %pad_maximum_fusion.2.refs_8_), channel_id=1, source_target_pairs={{0,2},{1,7},{2,4},{3,1},{4,6},{5,3},{6,0},{7,5},{8,10},{9,15},{10,... | collective-permute-start | bytes 1376264 | tf_op jit(solution)/shard_map/ppermute | solution.py:29
  27.1 3.3 %collective-permute-start.6 = (bf16[32,7168]{1,0:T(8,128)(2,1)}, bf16[32,7168]{1,0:T(8,128)(2,1)}, u32[]{:S(2)}, u32[]{:S(2)}) collective-permute-start(bf16[32,7168]{1,0:T(8,128)(2,1)} %collective-permute-done.1.refs_1_), channel_id=1, source_target_pairs={{0,2},{1,7},{2,4},{3,1},{4,6},{5,3},{6,0},{7,5},{8,10},{9,15},{10,... | collective-permute-start | bytes 1376264 | tf_op jit(solution)/shard_map/ppermute | solution.py:29
  32.1 3.3 %collective-permute-start.9 = (bf16[32,7168]{1,0:T(8,128)(2,1)}, bf16[32,7168]{1,0:T(8,128)(2,1)}, u32[]{:S(2)}, u32[]{:S(2)}) collective-permute-start(bf16[32,7168]{1,0:T(8,128)(2,1)} %collective-permute-done.7.refs_9_), channel_id=1, source_target_pairs={{0,2},{1,7},{2,4},{3,1},{4,6},{5,3},{6,0},{7,5},{8,10},{9,15},{10,... | collective-permute-start | bytes 1376264 | tf_op jit(solution)/shard_map/ppermute | solution.py:29
  37.0 3.3 %collective-permute-start.8 = (bf16[32,7168]{1,0:T(8,128)(2,1)}, bf16[32,7168]{1,0:T(8,128)(2,1)}, u32[]{:S(2)}, u32[]{:S(2)}) collective-permute-start(bf16[32,7168]{1,0:T(8,128)(2,1)} %collective-permute-done.6.refs_2_), channel_id=1, source_target_pairs={{0,2},{1,7},{2,4},{3,1},{4,6},{5,3},{6,0},{7,5},{8,10},{9,15},{10,... | collective-permute-start | bytes 1376264 | tf_op jit(solution)/shard_map/ppermute | solution.py:29
  41.9 3.3 %collective-permute-start.10 = (bf16[32,7168]{1,0:T(8,128)(2,1)}, bf16[32,7168]{1,0:T(8,128)(2,1)}, u32[]{:S(2)}, u32[]{:S(2)}) collective-permute-start(bf16[32,7168]{1,0:T(8,128)(2,1)} %collective-permute-done.9.refs_10_), channel_id=1, source_target_pairs={{0,2},{1,7},{2,4},{3,1},{4,6},{5,3},{6,0},{7,5},{8,10},{9,15},{10,... | collective-permute-start | bytes 1376264 | tf_op jit(solution)/shard_map/ppermute | solution.py:29
  45.2 1.8 %collective-permute-start.13 = (bf16[64,7296]{1,0:T(8,128)(2,1)S(1)}, bf16[64,7296]{1,0:T(8,128)(2,1)}, u32[]{:S(2)}, u32[]{:S(2)}) collective-permute-start(bf16[64,7296]{1,0:T(8,128)(2,1)S(1)} %collective-permute-done.11.refs_1_.refs_5_), channel_id=1, source_target_pairs={{0,1},{1,0},{2,3},{3,2},{4,5},{5,4},{6,7},{7,6},{8,9},{9,8},{10,11... | collective-permute-start | bytes 2801672 | tf_op jit(solution)/shard_map/ppermute | solution.py:29
  47.0 2.2 %collective-permute-done.13.refs_3_.refs_7_ = bf16[64,7296]{1,0:T(8,128)(2,1)} collective-permute-done((bf16[64,7296]{1,0:T(8,128)(2,1)S(1)}, bf16[64,7296]{1,0:T(8,128)(2,1)}, u32[]{:S(2)}, u32[]{:S(2)}) %collective-permute-start.13) | collective-permute-done | bytes 933920 | tf_op jit(solution)/shard_map/ppermute | solution.py:29
  49.2 9.9 %shard_map.104 = (bf16[64,7168]{1,0:T(8,128)(2,1)S(1)}, bf16[64,7168]{1,0:T(8,128)(2,1)S(1)}, bf16[64,7168]{1,0:T(8,128)(2,1)S(1)}, bf16[64,7168]{1,0:T(8,128)(2,1)S(1)}) custom-call(bf16[64,7296]{1,0:T(8,128)(2,1)S(1)} %pad_maximum_fusion.refs_0_.refs_4_, bf16[64,7296]{1,0:T(8,128)(2,1)S(1)} %collective-permute-done.11.refs_1_.refs_5_, ...), custom_call_target="tpu_custom_call" | custom-call | flops 2818572288 | bytes 18350080 | tf_op jit(solution)/shard_map/pallas_call | solution.py:239
  67.2 12.2 %shard_map.105 = (bf16[16,7168]{1,0:T(8,128)(2,1)S(1)}, bf16[16,7168]{1,0:T(8,128)(2,1)S(1)}, bf16[16,7168]{1,0:T(8,128)(2,1)S(1)}, bf16[16,7168]{1,0:T(8,128)(2...) custom-call(bf16[32,7168]{1,0:T(8,128)(2,1)S(1)} %pad_maximum_fusion, ...), custom_call_target="tpu_custom_call" | custom-call | flops 4697620480 | bytes 25690112 | tf_op jit(solution)/shard_map/pallas_call | solution.py:239
  80.1 2.1 %collective-permute-done.25 = bf16[64,7168]{1,0:T(8,128)(2,1)S(1)} collective-permute-done((bf16[64,7168]{1,0:T(8,128)(2,1)S(1)}, bf16[64,7168]{1,0:T(8,128)(2,1)S(1)}, u32[]{:S(2)}, u32[]{:S(2)}) %collective-permute-start.25) | collective-permute-done | bytes 917536 | tf_op jit(solution)/shard_map/ppermute | solution.py:29
  83.1 3.1 %collective-permute-start.14 = (bf16[64,7168]{1,0:T(8,128)(2,1)S(1)}, bf16[64,7168]{1,0:T(8,128)(2,1)S(1)}, u32[]{:S(2)}, u32[]{:S(2)}) collective-permute-start(bf16[64,7168]{1,0:T(8,128)(2,1)S(1)} %get-tuple-element.66), channel_id=1, source_target_pairs={{0,1},{1,0},{2,3},{3,2},{4,5},{5,4},{6,7},{7,6},{8,9},{9,8},{10,11... | collective-permute-start | bytes 2752520 | tf_op jit(solution)/shard_map/ppermute | solution.py:29
  89.1 4.9 %collective-permute-done.27 = bf16[16,7168]{1,0:T(8,128)(2,1)S(1)} collective-permute-done((bf16[16,7168]{1,0:T(8,128)(2,1)S(1)}, bf16[16,7168]{1,0:T(8,128)(2,1)S(1)}, u32[]{:S(2)}, u32[]{:S(2)}) %collective-permute-start.27) | collective-permute-done | bytes 229408 | tf_op jit(solution)/shard_map/ppermute | solution.py:29
  94.4 4.9 %collective-permute-done.26 = bf16[32,7168]{1,0:T(8,128)(2,1)S(1)} collective-permute-done((bf16[32,7168]{1,0:T(8,128)(2,1)S(1)}, bf16[32,7168]{1,0:T(8,128)(2,1)S(1)}, u32[]{:S(2)}, u32[]{:S(2)}) %collective-permute-start.26) | collective-permute-done | bytes 458784 | tf_op jit(solution)/shard_map/ppermute | solution.py:29
  102.8 2.0 %collective-permute-start.38 = (bf16[16,7168]{1,0:T(8,128)(2,1)S(1)}, bf16[16,7168]{1,0:T(8,128)(2,1)S(1)}, u32[]{:S(2)}, u32[]{:S(2)}) collective-permute-start(bf16[16,7168]{1,0:T(8,128)(2,1)S(1)} %add_convert_fusion.3), channel_id=1, source_target_pairs={{0,6},{1,3},{2,0},{3,5},{4,2},{5,7},{6,4},{7,1},{8,14},{9,11},{10,... | collective-permute-start | bytes 688136 | tf_op jit(solution)/shard_map/ppermute | solution.py:29
  104.8 4.2 %collective-permute-done.33 = bf16[16,7168]{1,0:T(8,128)(2,1)S(1)} collective-permute-done((bf16[16,7168]{1,0:T(8,128)(2,1)S(1)}, bf16[16,7168]{1,0:T(8,128)(2,1)S(1)}, u32[]{:S(2)}, u32[]{:S(2)}) %collective-permute-start.33) | collective-permute-done | bytes 229408 | tf_op jit(solution)/shard_map/ppermute | solution.py:29
  109.0 5.5 %collective-permute-done.32 = bf16[16,7168]{1,0:T(8,128)(2,1)S(1)} collective-permute-done((bf16[16,7168]{1,0:T(8,128)(2,1)S(1)}, bf16[16,7168]{1,0:T(8,128)(2,1)S(1)}, u32[]{:S(2)}, u32[]{:S(2)}) %collective-permute-start.32) | collective-permute-done | bytes 229408 | tf_op jit(solution)/shard_map/ppermute | solution.py:29
  116.9 5.7 %collective-permute-start.37 = (bf16[16,7168]{1,0:T(8,128)(2,1)S(1)}, bf16[16,7168]{1,0:T(8,128)(2,1)S(1)}, u32[]{:S(2)}, u32[]{:S(2)}) collective-permute-start(bf16[16,7168]{1,0:T(8,128)(2,1)S(1)} %add_convert_fusion.2), channel_id=1, source_target_pairs={{0,240},{1,241},{2,242},{3,243},{4,244},{5,245},{6,246},{7,247},{8... | collective-permute-start | bytes 688136 | tf_op jit(solution)/shard_map/ppermute | solution.py:76
  122.7 3.2 %collective-permute-start.39 = (bf16[16,7168]{1,0:T(8,128)(2,1)S(1)}, bf16[16,7168]{1,0:T(8,128)(2,1)S(1)}, u32[]{:S(2)}, u32[]{:S(2)}) collective-permute-start(bf16[16,7168]{1,0:T(8,128)(2,1)S(1)} %add_convert_fusion.1), channel_id=1, source_target_pairs={{0,248},{1,249},{2,250},{3,251},{4,252},{5,253},{6,254},{7,255},{8... | collective-permute-start | bytes 688136 | tf_op jit(solution)/shard_map/ppermute | solution.py:76
  125.9 3.2 %collective-permute-done.37 = bf16[16,7168]{1,0:T(8,128)(2,1)S(1)} collective-permute-done((bf16[16,7168]{1,0:T(8,128)(2,1)S(1)}, bf16[16,7168]{1,0:T(8,128)(2,1)S(1)}, u32[]{:S(2)}, u32[]{:S(2)}) %collective-permute-start.37) | collective-permute-done | bytes 229408 | tf_op jit(solution)/shard_map/ppermute | solution.py:76
  129.1 2.8 %collective-permute-done.39 = bf16[16,7168]{1,0:T(8,128)(2,1)S(1)} collective-permute-done((bf16[16,7168]{1,0:T(8,128)(2,1)S(1)}, bf16[16,7168]{1,0:T(8,128)(2,1)S(1)}, u32[]{:S(2)}, u32[]{:S(2)}) %collective-permute-start.39) | collective-permute-done | bytes 229408 | tf_op jit(solution)/shard_map/ppermute | solution.py:76
  (98 shorter events, 34.4 us)
Async XLA Ops:
  2.6 10.6 %collective-permute-start = (bf16[16,7168]{1,0:T(8,128)(2,1)S(1)}, bf16[16,7168]{1,0:T(8,128)(2,1)S(1)}, u32[]{:S(2)}, u32[]{:S(2)}) collective-permute-start(bf16[16,7168]{1,0:T(8,128)(2,1)S(1)} %get-tuple-element.119), channel_id=1, source_target_pairs={{0,8},{1,9},{2,10},{3,11},{4,12},{5,13},{6,14},{7,15},{8,0},{9,1},... | collective-permute-start | bytes 688136 | tf_op jit(solution)/shard_map/ppermute | solution.py:29
  9.3 10.4 %collective-permute-start.4 = (bf16[16,7296]{1,0:T(8,128)(2,1)S(1)}, bf16[16,7296]{1,0:T(8,128)(2,1)S(1)}, u32[]{:S(2)}, u32[]{:S(2)}) collective-permute-start(bf16[16,7296]{1,0:T(8,128)(2,1)S(1)} %pad_maximum_fusion.3), channel_id=1, source_target_pairs={{0,4},{1,5},{2,6},{3,7},{4,0},{5,1},{6,2},{7,3},{8,12},{9,13},{10,... | collective-permute-start | bytes 700424 | tf_op jit(solution)/shard_map/ppermute | solution.py:29
  11.9 10.2 %collective-permute-start.3 = (bf16[16,7296]{1,0:T(8,128)(2,1)S(1)}, bf16[16,7296]{1,0:T(8,128)(2,1)S(1)}, u32[]{:S(2)}, u32[]{:S(2)}) collective-permute-start(bf16[16,7296]{1,0:T(8,128)(2,1)S(1)} %pad_maximum_fusion.3), channel_id=1, source_target_pairs={{0,2},{1,7},{2,4},{3,1},{4,6},{5,3},{6,0},{7,5},{8,10},{9,15},{10,... | collective-permute-start | bytes 700424 | tf_op jit(solution)/shard_map/ppermute | solution.py:29
  13.0 9.2 %collective-permute-start.2 = (bf16[16,7168]{1,0:T(8,128)(2,1)S(1)}, bf16[16,7168]{1,0:T(8,128)(2,1)S(1)}, u32[]{:S(2)}, u32[]{:S(2)}) collective-permute-start(bf16[16,7168]{1,0:T(8,128)(2,1)S(1)} %get-tuple-element.116), channel_id=1, source_target_pairs={{0,8},{1,9},{2,10},{3,11},{4,12},{5,13},{6,14},{7,15},{8,0},{9,1},... | collective-permute-start | bytes 688136 | tf_op jit(solution)/shard_map/ppermute | solution.py:29
  13.2 13.9 %collective-permute-start.1 = (bf16[32,7168]{1,0:T(8,128)(2,1)S(1)}, bf16[32,7168]{1,0:T(8,128)(2,1)}, u32[]{:S(2)}, u32[]{:S(2)}) collective-permute-start(bf16[32,7168]{1,0:T(8,128)(2,1)S(1)} %pad_maximum_fusion.1.refs_0_), channel_id=1, source_target_pairs={{0,2},{1,7},{2,4},{3,1},{4,6},{5,3},{6,0},{7,5},{8,10},{9,15},{10,... | collective-permute-start | bytes 1376264 | tf_op jit(solution)/shard_map/ppermute | solution.py:29
  22.2 23.0 %collective-permute-start.11 = (bf16[64,7296]{1,0:T(8,128)(2,1)S(1)}, bf16[64,7296]{1,0:T(8,128)(2,1)S(1)}, u32[]{:S(2)}, u32[]{:S(2)}) collective-permute-start(bf16[64,7296]{1,0:T(8,128)(2,1)S(1)} %pad_maximum_fusion.refs_0_.refs_4_), channel_id=1, source_target_pairs={{0,8},{1,9},{2,10},{3,11},{4,12},{5,13},{6,14},{7,15},{8,0},{9,1},... | collective-permute-start | bytes 2801672 | tf_op jit(solution)/shard_map/ppermute | solution.py:29
  22.4 9.7 %collective-permute-start.7 = (bf16[32,7168]{1,0:T(8,128)(2,1)S(1)}, bf16[32,7168]{1,0:T(8,128)(2,1)}, u32[]{:S(2)}, u32[]{:S(2)}) collective-permute-start(bf16[32,7168]{1,0:T(8,128)(2,1)S(1)} %pad_maximum_fusion.2.refs_8_), channel_id=1, source_target_pairs={{0,2},{1,7},{2,4},{3,1},{4,6},{5,3},{6,0},{7,5},{8,10},{9,15},{10,... | collective-permute-start | bytes 1376264 | tf_op jit(solution)/shard_map/ppermute | solution.py:29
  27.1 9.8 %collective-permute-start.6 = (bf16[32,7168]{1,0:T(8,128)(2,1)}, bf16[32,7168]{1,0:T(8,128)(2,1)}, u32[]{:S(2)}, u32[]{:S(2)}) collective-permute-start(bf16[32,7168]{1,0:T(8,128)(2,1)} %collective-permute-done.1.refs_1_), channel_id=1, source_target_pairs={{0,2},{1,7},{2,4},{3,1},{4,6},{5,3},{6,0},{7,5},{8,10},{9,15},{10,... | collective-permute-start | bytes 1376264 | tf_op jit(solution)/shard_map/ppermute | solution.py:29
  32.1 9.8 %collective-permute-start.9 = (bf16[32,7168]{1,0:T(8,128)(2,1)}, bf16[32,7168]{1,0:T(8,128)(2,1)}, u32[]{:S(2)}, u32[]{:S(2)}) collective-permute-start(bf16[32,7168]{1,0:T(8,128)(2,1)} %collective-permute-done.7.refs_9_), channel_id=1, source_target_pairs={{0,2},{1,7},{2,4},{3,1},{4,6},{5,3},{6,0},{7,5},{8,10},{9,15},{10,... | collective-permute-start | bytes 1376264 | tf_op jit(solution)/shard_map/ppermute | solution.py:29
  35.4 13.8 %collective-permute-start.12 = (bf16[64,7296]{1,0:T(8,128)(2,1)S(1)}, bf16[64,7296]{1,0:T(8,128)(2,1)S(1)}, u32[]{:S(2)}, u32[]{:S(2)}) collective-permute-start(bf16[64,7296]{1,0:T(8,128)(2,1)S(1)} %pad_maximum_fusion.refs_0_.refs_4_), channel_id=1, source_target_pairs={{0,1},{1,0},{2,3},{3,2},{4,5},{5,4},{6,7},{7,6},{8,9},{9,8},{10,11... | collective-permute-start | bytes 2801672 | tf_op jit(solution)/shard_map/ppermute | solution.py:29
  37.0 22.1 %collective-permute-start.8 = (bf16[32,7168]{1,0:T(8,128)(2,1)}, bf16[32,7168]{1,0:T(8,128)(2,1)}, u32[]{:S(2)}, u32[]{:S(2)}) collective-permute-start(bf16[32,7168]{1,0:T(8,128)(2,1)} %collective-permute-done.6.refs_2_), channel_id=1, source_target_pairs={{0,2},{1,7},{2,4},{3,1},{4,6},{5,3},{6,0},{7,5},{8,10},{9,15},{10,... | collective-permute-start | bytes 1376264 | tf_op jit(solution)/shard_map/ppermute | solution.py:29
  41.9 17.2 %collective-permute-start.10 = (bf16[32,7168]{1,0:T(8,128)(2,1)}, bf16[32,7168]{1,0:T(8,128)(2,1)}, u32[]{:S(2)}, u32[]{:S(2)}) collective-permute-start(bf16[32,7168]{1,0:T(8,128)(2,1)} %collective-permute-done.9.refs_10_), channel_id=1, source_target_pairs={{0,2},{1,7},{2,4},{3,1},{4,6},{5,3},{6,0},{7,5},{8,10},{9,15},{10,... | collective-permute-start | bytes 1376264 | tf_op jit(solution)/shard_map/ppermute | solution.py:29
  65.6 13.8 %collective-permute-start.18 = (bf16[32,7168]{1,0:T(8,128)(2,1)S(1)}, bf16[32,7168]{1,0:T(8,128)(2,1)S(1)}, u32[]{:S(2)}, u32[]{:S(2)}) collective-permute-start(bf16[32,7168]{1,0:T(8,128)(2,1)S(1)} %get-tuple-element.71), channel_id=1, source_target_pairs={{0,8},{1,9},{2,10},{3,11},{4,12},{5,13},{6,14},{7,15},{8,0},{9,1},... | collective-permute-start | bytes 1376264 | tf_op jit(solution)/shard_map/ppermute | solution.py:29
  83.1 16.1 %collective-permute-start.14 = (bf16[64,7168]{1,0:T(8,128)(2,1)S(1)}, bf16[64,7168]{1,0:T(8,128)(2,1)S(1)}, u32[]{:S(2)}, u32[]{:S(2)}) collective-permute-start(bf16[64,7168]{1,0:T(8,128)(2,1)S(1)} %get-tuple-element.66), channel_id=1, source_target_pairs={{0,1},{1,0},{2,3},{3,2},{4,5},{5,4},{6,7},{7,6},{8,9},{9,8},{10,11... | collective-permute-start | bytes 2752520 | tf_op jit(solution)/shard_map/ppermute | solution.py:29
  86.2 16.1 %collective-permute-start.31 = (bf16[64,7168]{1,0:T(8,128)(2,1)S(1)}, bf16[64,7168]{1,0:T(8,128)(2,1)S(1)}, u32[]{:S(2)}, u32[]{:S(2)}) collective-permute-start(bf16[64,7168]{1,0:T(8,128)(2,1)S(1)} %get-tuple-element.98), channel_id=1, source_target_pairs={{0,1},{1,0},{2,3},{3,2},{4,5},{5,4},{6,7},{7,6},{8,9},{9,8},{10,11... | collective-permute-start | bytes 2752520 | tf_op jit(solution)/shard_map/ppermute | solution.py:29
  86.2 13.1 %collective-permute-start.26 = (bf16[32,7168]{1,0:T(8,128)(2,1)S(1)}, bf16[32,7168]{1,0:T(8,128)(2,1)S(1)}, u32[]{:S(2)}, u32[]{:S(2)}) collective-permute-start(bf16[32,7168]{1,0:T(8,128)(2,1)S(1)} %get-tuple-element.88), channel_id=1, source_target_pairs={{0,8},{1,9},{2,10},{3,11},{4,12},{5,13},{6,14},{7,15},{8,0},{9,1},... | collective-permute-start | bytes 1376264 | tf_op jit(solution)/shard_map/ppermute | solution.py:29
  89.0 12.4 %collective-permute-start.30 = (bf16[16,7168]{1,0:T(8,128)(2,1)S(1)}, bf16[16,7168]{1,0:T(8,128)(2,1)S(1)}, u32[]{:S(2)}, u32[]{:S(2)}) collective-permute-start(bf16[16,7168]{1,0:T(8,128)(2,1)S(1)} %add_convert_fusion.6), channel_id=1, source_target_pairs={{0,6},{1,3},{2,0},{3,5},{4,2},{5,7},{6,4},{7,1},{8,14},{9,11},{10,... | collective-permute-start | bytes 688136 | tf_op jit(solution)/shard_map/ppermute | solution.py:29
  99.9 9.1 %collective-permute-start.33 = (bf16[16,7168]{1,0:T(8,128)(2,1)S(1)}, bf16[16,7168]{1,0:T(8,128)(2,1)S(1)}, u32[]{:S(2)}, u32[]{:S(2)}) collective-permute-start(bf16[16,7168]{1,0:T(8,128)(2,1)S(1)} %get-tuple-element.110), channel_id=1, source_target_pairs={{0,4},{1,5},{2,6},{3,7},{4,0},{5,1},{6,2},{7,3},{8,12},{9,13},{10,... | collective-permute-start | bytes 688136 | tf_op jit(solution)/shard_map/ppermute | solution.py:29
  101.5 13.0 %collective-permute-start.32 = (bf16[16,7168]{1,0:T(8,128)(2,1)S(1)}, bf16[16,7168]{1,0:T(8,128)(2,1)S(1)}, u32[]{:S(2)}, u32[]{:S(2)}) collective-permute-start(bf16[16,7168]{1,0:T(8,128)(2,1)S(1)} %get-tuple-element.108), channel_id=1, source_target_pairs={{0,6},{1,3},{2,0},{3,5},{4,2},{5,7},{6,4},{7,1},{8,14},{9,11},{10,... | collective-permute-start | bytes 688136 | tf_op jit(solution)/shard_map/ppermute | solution.py:29
  102.3 14.4 %collective-permute-start.36 = (bf16[16,7168]{1,0:T(8,128)(2,1)S(1)}, bf16[16,7168]{1,0:T(8,128)(2,1)S(1)}, u32[]{:S(2)}, u32[]{:S(2)}) collective-permute-start(bf16[16,7168]{1,0:T(8,128)(2,1)S(1)} %add_convert_fusion.4), channel_id=1, source_target_pairs={{0,6},{1,3},{2,0},{3,5},{4,2},{5,7},{6,4},{7,1},{8,14},{9,11},{10,... | collective-permute-start | bytes 688136 | tf_op jit(solution)/shard_map/ppermute | solution.py:29
  102.8 19.7 %collective-permute-start.38 = (bf16[16,7168]{1,0:T(8,128)(2,1)S(1)}, bf16[16,7168]{1,0:T(8,128)(2,1)S(1)}, u32[]{:S(2)}, u32[]{:S(2)}) collective-permute-start(bf16[16,7168]{1,0:T(8,128)(2,1)S(1)} %add_convert_fusion.3), channel_id=1, source_target_pairs={{0,6},{1,3},{2,0},{3,5},{4,2},{5,7},{6,4},{7,1},{8,14},{9,11},{10,... | collective-permute-start | bytes 688136 | tf_op jit(solution)/shard_map/ppermute | solution.py:29
  114.7 11.2 %collective-permute-start.35 = (bf16[16,7168]{1,0:T(8,128)(2,1)S(1)}, bf16[16,7168]{1,0:T(8,128)(2,1)S(1)}, u32[]{:S(2)}, u32[]{:S(2)}) collective-permute-start(bf16[16,7168]{1,0:T(8,128)(2,1)S(1)} %fusion.3), channel_id=1, source_target_pairs={{0,16},{1,17},{2,18},{3,19},{4,20},{5,21},{6,22},{7,23},{8,24},{9,... | collective-permute-start | bytes 688136 | tf_op jit(solution)/shard_map/ppermute | solution.py:76
  116.9 12.3 %collective-permute-start.37 = (bf16[16,7168]{1,0:T(8,128)(2,1)S(1)}, bf16[16,7168]{1,0:T(8,128)(2,1)S(1)}, u32[]{:S(2)}, u32[]{:S(2)}) collective-permute-start(bf16[16,7168]{1,0:T(8,128)(2,1)S(1)} %add_convert_fusion.2), channel_id=1, source_target_pairs={{0,240},{1,241},{2,242},{3,243},{4,244},{5,245},{6,246},{7,247},{8... | collective-permute-start | bytes 688136 | tf_op jit(solution)/shard_map/ppermute | solution.py:76
  122.7 9.3 %collective-permute-start.39 = (bf16[16,7168]{1,0:T(8,128)(2,1)S(1)}, bf16[16,7168]{1,0:T(8,128)(2,1)S(1)}, u32[]{:S(2)}, u32[]{:S(2)}) collective-permute-start(bf16[16,7168]{1,0:T(8,128)(2,1)S(1)} %add_convert_fusion.1), channel_id=1, source_target_pairs={{0,248},{1,249},{2,250},{3,251},{4,252},{5,253},{6,254},{7,255},{8... | collective-permute-start | bytes 688136 | tf_op jit(solution)/shard_map/ppermute | solution.py:76
  (24 other events, 218.0 us)
